TPU v7x, 256 devices: a whole 4x4x8 slice. The times are simulated.
256 devices in a mesh: mem: 16 (over z, core), tile: 16 (over x, y).
Axes of the slice: x: 4, y: 4, z: 8, core: 2. Of those that a mesh axis runs over, the one named last changes fastest.
Arguments:
- members: float32 [512, 2, 512, 128], P('mem', None, 'tile'), may hold values from -6 to 6
- courant: float32 [2, 128], replicated, may hold values from 0.2 to 0.9
- obs_cell: int32 [4096], P('tile'), may hold values from 0 to 8191
- obs_value: float32 [4096], P('tile'), may hold values from -6 to 6
- obs_rinv: float32 [4096], P('tile'), may hold values from 0.3 to 3
- nbr_obs: int32 [512, 512], P(('tile', 'mem')), may hold values from 0 to 4095, as said below
- nbr_class: int32 [512, 512], P(('tile', 'mem')), may hold values from 0 to 15
- nbr_count: int32 [512], P(('tile', 'mem')), may hold values from 128 to 512, as said below
- loc_table: float32 [16], replicated, may hold values from 0.2 to 1
Outputs:
- analysis: float32 [512, 2, 512, 128], P('mem', None, 'tile')
Inputs may be any that keep to these rules, and one draw needn't show every extreme that they name: nbr_obs[g] names observations of the tile of longitude line g or of the tiles just west and east of it (periodic); an observation may be named more than once. Only the first nbr_count[g] slots of patch g are used.
All inputs are finite; a program needn't handle non-finite values. Where the computation divides by a largest or mean magnitude, that divisor is 1e-20 or more.
Results may differ from a plain program's by a relative error of at most 0.0003.
Values sent between devices are 32-bit elements; how exact they have to be, the bound alone decides.
No kernel may reach another device: no remote copies, remote signals or barrier semaphores. Data moves between devices by JAX's collectives and lax.ppermute only.
A program may use at most 64 MiB of HBM per device.

v0:
```python
import functools
import jax
import jax.numpy as jnp
from jax import lax
from jax.experimental import pallas as pl
from jax.experimental.pallas import tpu as pltpu
from jax.sharding import PartitionSpec as P

NSTEP = 2
NS_ITERS = 8
DIFFUSE = 0.1
HALF = 256
PAD = 16
NARROW = 32.0
SMALL, MID, LOW = 1.0 / 5, 1.0 / 32, 1.0 / 1024
BF = jnp.bfloat16
F32 = jnp.float32
LO, HI = slice(0, HALF), slice(HALF, 2 * HALF)


def split(value):
    high = value.astype(BF)
    return high, (value - high.astype(F32)).astype(BF)


def mm(left, right):
    return jnp.dot(left, right, preferred_element_type=F32)


def mm_t(left, right):
    return lax.dot_general(left, right, (((1,), (1,)), ((), ())), preferred_element_type=F32)


def root_kernel(near_ref, own_ref, far_ref, wsum_ref, out_ref, rhs_ref, bh, bl, t, p, ph, pl_, gh, gl, z, zh, zl):
    devices, _, obs_tile = own_ref.shape
    patches, members = out_ref.shape[:2]
    mem_dev = members // devices
    inv = 1.0 / (members - 1)
    top = 2 * PAD
    eye = (
        lax.broadcasted_iota(jnp.int32, (HALF, HALF), 0)
        == lax.broadcasted_iota(jnp.int32, (HALF, HALF), 1)
    ).astype(F32)

    def put(value, full, high, low, n, rows, cols):
        if full is not None:
            full[n, rows, cols] = value
        high[n, rows, cols], low[n, rows, cols] = split(value)

    def gram(n):
        for j, ref in enumerate((near_ref, own_ref, far_ref)):
            spot = slice(j * obs_tile, (j + 1) * obs_tile)
            block = ref[:, 0:mem_dev, :].reshape(members, obs_tile)
            mean = jnp.sum(block, axis=0, keepdims=True) * (1.0 / members)
            value = ref[0, mem_dev : mem_dev + 1, :]
            total = ref[0, mem_dev + 1 : mem_dev + 2, :] * wsum_ref[n : n + 1, spot]
            root = jnp.where(total > 0.0, jnp.sqrt(jnp.maximum(total, 1e-30)), 0.0)
            row = jnp.broadcast_to(root * (value - mean), (PAD, obs_tile))
            bh[n, 0:PAD, spot], bh[n, PAD:top, spot] = split(row)
            bh[n, top:, spot], bl[n, :, spot] = split((block - mean) * root)
        first = bh[n, 0 : top + HALF, :]
        second = bh[n, top + HALF :, :]
        left = mm_t(first, first[top:, :])
        right = mm_t(first, second)
        left_low = mm_t(first, bl[n, LO, :])
        right_low = mm_t(first, bl[n, HI, :])
        t[n, LO, LO] = 0.5 * left[top:] + left_low[top:]
        t[n, LO, HI] = right[top:] + right_low[top:]
        rhs0 = (left[0:1] + left[PAD : PAD + 1] + left_low[0:1]) * inv
        rhs1 = (right[0:1] + right[PAD : PAD + 1] + right_low[0:1]) * inv
        rhs_ref[n, :, LO] = jnp.broadcast_to(rhs0, (8, HALF))
        rhs_ref[n, :, HI] = jnp.broadcast_to(rhs1, (8, HALF))
        t[n, HI, LO] = mm_t(second, bl[n, LO, :])
        t[n, HI, HI] = 0.5 * mm_t(second, second) + mm_t(second, bl[n, HI, :])

    def start(n):
        g00 = (t[n, LO, LO] + t[n, LO, LO].T) * inv + eye
        g01 = (t[n, LO, HI] + t[n, HI, LO].T) * inv
        g11 = (t[n, HI, HI] + t[n, HI, HI].T) * inv + eye
        g10 = g01.T
        rows0 = jnp.sum(jnp.abs(g00), 0, keepdims=True) + jnp.sum(jnp.abs(g10), 0, keepdims=True)
        rows1 = jnp.sum(jnp.abs(g01), 0, keepdims=True) + jnp.sum(jnp.abs(g11), 0, keepdims=True)
        scale = jnp.max(jnp.maximum(rows0, rows1), axis=1, keepdims=True)
        shrink = 1.0 / scale
        for rows, cols, g in ((LO, LO, g00), (LO, HI, g01), (HI, LO, g10), (HI, HI, g11)):
            cur = g * shrink
            put(cur, p, ph, pl_, n, rows, cols)
            first = -0.5 * cur
            if rows == cols:
                first = first + 1.5 * eye
            put(first, z, zh, zl, n, rows, cols)
        return scale

    def square(n):
        t[n, LO, LO] = 0.5 * mm(ph[n, LO, :], ph[n, :, LO]) + mm(ph[n, LO, :], pl_[n, :, LO])
        t[n, HI, LO] = mm(ph[n, HI, :], ph[n, :, LO]) + mm(ph[n, HI, :], pl_[n, :, LO])
        t[n, LO, HI] = mm(ph[n, LO, :], pl_[n, :, HI])
        t[n, HI, HI] = 0.5 * mm(ph[n, HI, :], ph[n, :, HI]) + mm(ph[n, HI, :], pl_[n, :, HI])

    def squared(n, one_pass):
        g00 = t[n, LO, LO] + t[n, LO, LO].T
        g10 = t[n, HI, LO] + t[n, LO, HI].T
        g11 = t[n, HI, HI] + t[n, HI, HI].T
        for rows, cols, g in ((LO, LO, g00), (HI, LO, g10), (LO, HI, g10.T), (HI, HI, g11)):
            if one_pass:
                gh[n, rows, cols] = g.astype(BF)
            else:
                put(g, None, gh, gl, n, rows, cols)
        p[n, LO, LO] = 2.25 * p[n, LO, LO] - 1.5 * g00
        p[n, HI, LO] = 2.25 * p[n, HI, LO] - 1.5 * g10
        p[n, HI, HI] = 2.25 * p[n, HI, HI] - 1.5 * g11

    def product(n, high, low, rows, cols):
        return (
            mm(ph[n, rows, :], high[n, :, cols])
            + mm(pl_[n, rows, :], high[n, :, cols])
            + mm(ph[n, rows, :], low[n, :, cols])
        )

    def factor(n):
        z00 = 1.5 * z[n, LO, LO] - 0.5 * product(n, zh, zl, LO, LO)
        z10 = 1.5 * z[n, HI, LO] - 0.5 * product(n, zh, zl, HI, LO)
        z11 = 1.5 * z[n, HI, HI] - 0.5 * product(n, zh, zl, HI, HI)
        return z00, z10, z11

    def keep(n, parts):
        z00, z10, z11 = parts
        put(z00, z, zh, zl, n, LO, LO)
        put(z10, z, zh, zl, n, HI, LO)
        put(z10.T, None, zh, zl, n, LO, HI)
        put(z11, z, zh, zl, n, HI, HI)

    def cube(n, one_pass):
        def times(rows, cols):
            if one_pass:
                return mm(ph[n, rows, :], gh[n, :, cols])
            return product(n, gh, gl, rows, cols)

        n00 = p[n, LO, LO] + 0.25 * times(LO, LO)
        n10 = p[n, HI, LO] + 0.25 * times(HI, LO)
        n11 = p[n, HI, HI] + 0.25 * times(HI, HI)
        put(n00, p, ph, pl_, n, LO, LO)
        put(n10, p, ph, pl_, n, HI, LO)
        put(n10.T, None, ph, pl_, n, LO, HI)
        put(n11, p, ph, pl_, n, HI, HI)

    def sizes(n):
        p00, p10, p11 = p[n, LO, LO], p[n, HI, LO], p[n, HI, HI]
        total = jnp.sum(p00 * p00 + 2.0 * (p10 * p10) + p11 * p11) * (1.0 / members)
        trace = jnp.sum((p00 + p11) * eye) * (1.0 / members)
        return total, 1.0 - 2.0 * trace + total

    def widest():
        small, near = sizes(0)
        for n in range(1, patches):
            other_small, other_near = sizes(n)
            small, near = jnp.maximum(small, other_small), jnp.maximum(near, other_near)
        return small, near

    def near_one(n):
        e10 = -p[n, HI, LO]
        gh[n, LO, LO] = (eye - p[n, LO, LO]).astype(BF)
        gh[n, HI, LO] = e10.astype(BF)
        gh[n, LO, HI] = e10.T.astype(BF)
        gh[n, HI, HI] = (eye - p[n, HI, HI]).astype(BF)

    def near_factor(n):
        z00 = z[n, LO, LO] + 0.5 * mm(gh[n, LO, :], zh[n, :, LO])
        z10 = z[n, HI, LO] + 0.5 * mm(gh[n, HI, :], zh[n, :, LO])
        z11 = z[n, HI, HI] + 0.5 * mm(gh[n, HI, :], zh[n, :, HI])
        return z00, z10, z11

    def near_square(n):
        t[n, LO, LO] = mm(gh[n, LO, :], gh[n, :, LO])
        t[n, HI, LO] = mm(gh[n, HI, :], gh[n, :, LO])
        t[n, HI, HI] = mm(gh[n, HI, :], gh[n, :, HI])

    def near_squared(n):
        gl[n, LO, LO] = t[n, LO, LO].astype(BF)
        gl[n, HI, LO] = t[n, HI, LO].astype(BF)
        gl[n, LO, HI] = t[n, HI, LO].T.astype(BF)
        gl[n, HI, HI] = t[n, HI, HI].astype(BF)

    def near_cube(n):
        e00 = 0.75 * t[n, LO, LO] + 0.25 * mm(gh[n, LO, :], gl[n, :, LO])
        e10 = 0.75 * t[n, HI, LO] + 0.25 * mm(gh[n, HI, :], gl[n, :, LO])
        e11 = 0.75 * t[n, HI, HI] + 0.25 * mm(gh[n, HI, :], gl[n, :, HI])
        put(eye - e00, p, ph, pl_, n, LO, LO)
        put(-e10, p, ph, pl_, n, HI, LO)
        put(-e10.T, None, ph, pl_, n, LO, HI)
        put(eye - e11, p, ph, pl_, n, HI, HI)

    every = range(patches)
    for n in every:
        gram(n)
    scales = [start(n) for n in every]

    def sweep(first, one_pass):
        for n in every:
            square(n)
        for n in every:
            squared(n, one_pass)
            if not first:
                keep(n, factor(n))
            cube(n, one_pass)

    def near_sweep(one_pass):
        for n in every:
            near_one(n)
        for n in every:
            near_square(n)
        for n in every:
            near_squared(n)
            keep(n, near_factor(n) if one_pass else factor(n))
            near_cube(n)

    spread = jnp.max(jnp.concatenate(scales, 0))
    narrow = spread <= NARROW
    small, _ = widest()

    few = jnp.logical_and(small <= SMALL, narrow)

    @pl.when(jnp.logical_not(few))
    def _():
        sweep(True, False)

    @pl.when(few)
    def _():
        sweep(True, True)

    def step(_, carry):
        small, near = carry

        few = jnp.logical_and(small <= SMALL, narrow)
        rest = jnp.logical_not(few)

        @pl.when(few)
        def _():
            sweep(False, True)

        @pl.when(jnp.logical_and(rest, near > MID))
        def _():
            sweep(False, False)

        @pl.when(jnp.logical_and(rest, jnp.logical_and(near <= MID, near > LOW)))
        def _():
            near_sweep(False)

        @pl.when(jnp.logical_and(rest, near <= LOW))
        def _():
            near_sweep(True)

        return widest()

    _, near = lax.fori_loop(0, NS_ITERS - 2, step, widest())

    def finish(make):
        for n in every:
            z00, z10, z11 = make(n)
            out_ref[n, LO, LO] = z00 * lax.rsqrt(scales[n])
            out_ref[n, HI, LO] = z10 * lax.rsqrt(scales[n])
            out_ref[n, LO, HI] = z10.T * lax.rsqrt(scales[n])
            out_ref[n, HI, HI] = z11 * lax.rsqrt(scales[n])

    @pl.when(near > LOW)
    def _():
        finish(factor)

    @pl.when(near <= LOW)
    def _():
        for n in every:
            near_one(n)
        finish(near_factor)


def inverse_roots(near, own, far, wsum, members):
    patches, nobs = wsum.shape
    square = (patches, members, members)
    return pl.pallas_call(
        root_kernel,
        out_shape=(
            jax.ShapeDtypeStruct(square, F32),
            jax.ShapeDtypeStruct((patches, 8, members), F32),
        ),
        scratch_shapes=[
            pltpu.VMEM((patches, 2 * PAD + members, nobs), BF),
            pltpu.VMEM((patches, members, nobs), BF),
            pltpu.VMEM(square, F32),
            pltpu.VMEM(square, F32),
            pltpu.VMEM(square, BF),
            pltpu.VMEM(square, BF),
            pltpu.VMEM(square, BF),
            pltpu.VMEM(square, BF),
            pltpu.VMEM(square, F32),
            pltpu.VMEM(square, BF),
            pltpu.VMEM(square, BF),
        ],
        compiler_params=pltpu.CompilerParams(vmem_limit_bytes=28 * 1024 * 1024),
        cost_estimate=pl.CostEstimate(flops=25 * 10**9, bytes_accessed=4 * 10**6, transcendentals=0),
    )(near, own, far, wsum)


def apply_kernel(root_ref, rhs_ref, cols_ref, out_ref):
    devices, patches, levels, mem_dev, nlat = cols_ref.shape
    members = devices * mem_dev
    for n in range(patches):
        root = root_ref[n]
        high, low = split(root)
        weight = jnp.sum(root * rhs_ref[n, 0:1, :], axis=1, keepdims=True)
        cols = jnp.concatenate(
            [cols_ref[:, n, lev].reshape(members, nlat) for lev in range(levels)], 1
        )
        center = jnp.sum(cols, axis=0, keepdims=True) * (1.0 / members)
        cols_high, cols_low = split(cols - center)
        moved = mm(high, cols_high) + mm(low, cols_high) + mm(high, cols_low)
        result = moved + (center + jnp.sum(moved * weight, axis=0, keepdims=True))
        for lev in range(levels):
            part = result[:, lev * nlat : (lev + 1) * nlat]
            out_ref[:, n, lev] = part.reshape(devices, mem_dev, nlat)


def apply_roots(roots, rhs, cols):
    return pl.pallas_call(
        apply_kernel,
        out_shape=jax.ShapeDtypeStruct(cols.shape, F32),
        compiler_params=pltpu.CompilerParams(vmem_limit_bytes=24 * 1024 * 1024),
        cost_estimate=pl.CostEstimate(flops=8 * 10**8, bytes_accessed=4 * 10**6, transcendentals=0),
    )(roots, rhs, cols)


def advance(field, west, courant):
    nlat = field.shape[1]
    lat = lax.broadcasted_iota(jnp.int32, field.shape, 1)
    upper = jnp.where(lat == nlat - 1, field, pltpu.roll(field, nlat - 1, 1))
    lower = jnp.where(lat == 0, field, pltpu.roll(field, 1, 1))
    return field - courant * (field - west) + DIFFUSE * (upper + lower - 2.0 * field)


def picker(cells, nlat):
    spot = (lax.broadcasted_iota(jnp.int32, (nlat, cells.shape[1]), 0) == cells % nlat).astype(BF)
    twice = jnp.concatenate([spot, spot], 0)
    return lambda value: mm(jnp.concatenate(split(value), 1), twice)


def inner_kernel(
    field_hbm, courant_hbm, cell_hbm, value_hbm, rinv_hbm, out_ref, edge_ref, message_ref, extra_ref,
    field_ref, courant_ref, cell_ref, value_ref, rinv_ref, sems
):
    copies = [
        pltpu.make_async_copy(source, target, sems.at[i])
        for i, (source, target) in enumerate(
            (
                (field_hbm, field_ref),
                (courant_hbm, courant_ref),
                (cell_hbm, cell_ref),
                (value_hbm, value_ref),
                (rinv_hbm, rinv_ref),
            )
        )
    ]
    for copy in copies:
        copy.start()
    for copy in copies:
        copy.wait()
    lines, levels, members, nlat = out_ref.shape
    cells = cell_ref[...]
    pick = picker(cells, nlat)
    source_row = cells // nlat
    obs = jnp.zeros((members, cells.shape[1]), F32)
    for lev in range(levels):
        courant = courant_ref[lev : lev + 1, :]
        old, old_next = None, None
        for line in range(lines):
            now = field_ref[pl.ds(lev * lines + line, members, stride=levels * lines), :]
            if line < NSTEP:
                edge_ref[line, lev] = now
            now_next = None
            if line >= 1:
                now_next = advance(now, old, courant)
            if line >= NSTEP:
                done = advance(now_next, old_next, courant)
                out_ref[line, lev] = done
                obs = jnp.where(source_row == lev * lines + line, pick(done), obs)
            old, old_next = now, now_next
    message_ref[0:members, :] = obs
    message_ref[members : members + 1, :] = value_ref[...]
    message_ref[members + 1 : members + 2, :] = rinv_ref[...]
    message_ref[members + 2 :, :] = jnp.zeros((6, obs.shape[1]), F32)
    extra_ref[...] = jnp.zeros(extra_ref.shape, jnp.int32)
    extra_ref[0:1, :] = cells
    edge_ref[NSTEP] = jnp.zeros(edge_ref.shape[1:], F32)
    for lev in range(levels):
        edge_ref[NSTEP, lev, 0:1, :] = courant_ref[lev : lev + 1, :]


def inner_forecast(members, courant, cells, value, rinv):
    mem_dev, levels, lines, nlat = members.shape
    rows = mem_dev * levels * lines
    nobs = cells.shape[1]
    return pl.pallas_call(
        inner_kernel,
        out_shape=(
            jax.ShapeDtypeStruct((lines, levels, mem_dev, nlat), F32),
            jax.ShapeDtypeStruct((NSTEP + 1, levels, mem_dev, nlat), F32),
            jax.ShapeDtypeStruct((mem_dev + 8, nobs), F32),
            jax.ShapeDtypeStruct((8, nobs), jnp.int32),
        ),
        in_specs=[pl.BlockSpec(memory_space=pltpu.HBM)] * 5,
        scratch_shapes=[
            pltpu.VMEM((rows, nlat), F32),
            pltpu.VMEM(courant.shape, F32),
            pltpu.VMEM(cells.shape, jnp.int32),
            pltpu.VMEM(value.shape, F32),
            pltpu.VMEM(rinv.shape, F32),
            pltpu.SemaphoreType.DMA((5,)),
        ],
        compiler_params=pltpu.CompilerParams(vmem_limit_bytes=60 * 1024 * 1024),
        cost_estimate=pl.CostEstimate(flops=10**8, bytes_accessed=2 * 10**6, transcendentals=0),
    )(members.reshape(rows, nlat), courant, cells, value, rinv)


def edge_kernel(lines, halo_ref, edge_ref, cell_ref, partial_ref, field_ref, out_ref, message_ref):
    del field_ref
    _, levels, members, nlat = edge_ref.shape
    cells = cell_ref[0:1, :]
    pick = picker(cells, nlat)
    source_row = cells // nlat
    obs = partial_ref[0:members, :]
    for lev in range(levels):
        courant = edge_ref[NSTEP, lev, 0:1, :]
        old = halo_ref[1, lev]
        old_next = advance(old, halo_ref[0, lev], courant)
        for line in range(NSTEP):
            now = edge_ref[line, lev]
            now_next = advance(now, old, courant)
            done = advance(now_next, old_next, courant)
            out_ref[line, lev] = done
            obs = jnp.where(source_row == lev * lines + line, pick(done), obs)
            old, old_next = now, now_next
    message_ref[0:members, :] = obs
    message_ref[members:, :] = partial_ref[members:, :]


def edge_forecast(halo, edge, cells, partial, field):
    lines, levels, mem_dev, nlat = field.shape

    def whole(array):
        zeros = (0,) * array.ndim
        return pl.BlockSpec(array.shape, lambda i: zeros)

    first = pl.BlockSpec((NSTEP, levels, mem_dev, nlat), lambda i: (0, 0, 0, 0))
    small = (halo, edge, cells, partial)
    return pl.pallas_call(
        functools.partial(edge_kernel, lines),
        grid=(1,),
        out_shape=(
            jax.ShapeDtypeStruct(field.shape, F32),
            jax.ShapeDtypeStruct(partial.shape, F32),
        ),
        in_specs=[whole(a) for a in small] + [pl.BlockSpec(memory_space=pl.ANY)],
        out_specs=(first, whole(partial)),
        input_output_aliases={len(small): 0},
        compiler_params=pltpu.CompilerParams(vmem_limit_bytes=60 * 1024 * 1024),
        cost_estimate=pl.CostEstimate(flops=10**7, bytes_accessed=10**6, transcendentals=0),
    )(*small, field)


def restore_kernel(part_ref, out_ref):
    devices, patches, levels, mem_dev, nlat = part_ref.shape
    lines = patches * devices
    for device in range(devices):
        for n in range(patches):
            for lev in range(levels):
                rows = pl.ds(lev * lines + patches * device + n, mem_dev, stride=levels * lines)
                out_ref[rows, :] = part_ref[device, n, lev]


def restore(parts):
    devices, patches, levels, mem_dev, nlat = parts.shape
    rows = mem_dev * levels * patches * devices
    out = pl.pallas_call(
        restore_kernel,
        out_shape=jax.ShapeDtypeStruct((rows, nlat), F32),
        compiler_params=pltpu.CompilerParams(vmem_limit_bytes=24 * 1024 * 1024),
    )(parts)
    return out.reshape(mem_dev, levels, patches * devices, nlat)


def shifted(value, axis, steps):
    count = lax.axis_size(axis)
    pairs = [(source, (source + steps) % count) for source in range(count)]
    return lax.ppermute(value, axis, pairs)


def neighbours(value):
    mem, tile = lax.axis_size("mem"), lax.axis_size("tile")
    pairs = [
        (m * tile + t, m * tile + (t + (1 if m % 2 == 0 else -1)) % tile)
        for m in range(mem)
        for t in range(tile)
    ]
    near = lax.ppermute(value, ("mem", "tile"), pairs)
    far = lax.ppermute(near, "mem", [(m, m ^ 1) for m in range(mem)])
    return near, far


def on_device(
    members, courant, obs_cell, obs_value, obs_rinv, nbr_obs, nbr_class, nbr_count, loc_table
):
    mem_dev, levels, lines, nlat = members.shape
    devices = lax.axis_size("mem")
    obs_tile = obs_cell.shape[0]
    slots = nbr_obs.shape[1]
    edge = jnp.transpose(members[:, :, lines - NSTEP :, :], (2, 1, 0, 3))
    halo = shifted(edge, "tile", 1)
    field, first_lines, partial, cells = inner_forecast(
        members, courant, obs_cell[None], obs_value[None], obs_rinv[None]
    )
    field, message = edge_forecast(halo, first_lines, cells, partial, field)
    own = lax.all_gather(message, "mem", axis=0, tiled=True)
    own, nbr_obs, nbr_class, nbr_count, loc_table, field = lax.optimization_barrier(
        (own, nbr_obs, nbr_class, nbr_count, loc_table, field)
    )
    near, far = neighbours(own)
    columns = lax.all_to_all(
        field.reshape(devices, lines // devices, levels, mem_dev, nlat), "mem", 0, 0, tiled=True
    )
    tile_index = lax.axis_index("tile")
    tile_count = lax.axis_size("tile")
    offset = (nbr_obs // obs_tile - tile_index + 1) % tile_count
    offset = jnp.where(lax.axis_index("mem") % 2 == 0, offset, 2 - offset)
    local_ids = offset * obs_tile + nbr_obs % obs_tile
    classes = jnp.arange(loc_table.shape[0])
    local_w = jnp.sum(jnp.where(nbr_class[..., None] == classes, loc_table, 0.0), -1)
    local_w = jnp.where(jnp.arange(slots) < nbr_count[:, None], local_w, 0.0)
    places = jnp.arange(3 * obs_tile)
    wsum = jnp.sum(jnp.where(local_ids[:, :, None] == places, local_w[:, :, None], 0.0), 1)

    shape = (devices, mem_dev + 8, obs_tile)
    roots, rhs = inverse_roots(
        near.reshape(shape), own.reshape(shape), far.reshape(shape), wsum, devices * mem_dev
    )
    parts = apply_roots(roots, rhs, columns)
    return restore(lax.all_to_all(parts, "mem", 0, 0, tiled=True))


def solution(mesh):
    return jax.shard_map(
        on_device,
        mesh=mesh,
        in_specs=(
            P("mem", None, "tile", None),
            P(),
            P("tile"),
            P("tile"),
            P("tile"),
            P(("tile", "mem"), None),
            P(("tile", "mem"), None),
            P(("tile", "mem")),
            P(),
        ),
        out_specs=P("mem", None, "tile", None),
        check_vma=False,
    )
```

profile of v0, /device:TPU:1, one launch (start us, length us, event | category | flops | bytes accessed | tf_op | source)
XLA Modules:
  0.0 113.4 jit_solution(11029689499692554390)
XLA Ops:
  0.0 1.0 slice.3
  1.0 2.2 %collective-permute-start = (f32[2,2,32,128]{3,2,1,0:T(8,128)S(1)}, f32[2,2,32,128]{3,2,1,0:T(8,128)S(1)}, u32[]{:S(2)}, u32[]{:S(2)}) collective-permute-start(f32[2,2,32,128]{3,2,1,0:T(8,128)S(1)} %bitcast.17), channel_id=1, source_target_pairs={{0,1},{1,2},{2,3},{3,4},{4,5},{5,6},{6,7},{7,8},{8,9},{9,10},{10,1... | collective-permute-start | bytes 196616 | tf_op jit(solution)/shard_map/ppermute | solution.py:492
  3.2 3.9 %shard_map.91 = (f32[32,2,32,128]{3,2,1,0:T(8,128)}, f32[3,2,32,128]{3,2,1,0:T(8,128)}, f32[40,256]{1,0:T(8,128)}, s32[8,256]{1,0:T(8,128)}) custom-call(f32[2048,128]{1,0:T(8,128)} %bitcast.16, f32[2,128]{1,0:T(2,128)} %courant_hbm.1, s32[1,256]{1,0:T(1,128)} %bitcast.18, f32[1,256]{1,0:T(1,128)} %bitcast.19, f32[1,256]{1,0:T(1,128)} %bitcast.20), custom_call_target="tpu_custom_call" | custom-call | flops 100000000 | bytes 2000000 | tf_op jit(solution)/shard_map/pallas_call | solution.py:400
  7.1 0.0 copy-start.5
  7.1 0.0 copy-start.7
  7.1 0.0 copy-start.6
  7.1 0.0 copy-start.8
  7.2 1.3 %collective-permute-done.halo_ref = f32[2,2,32,128]{3,2,1,0:T(8,128)S(1)} collective-permute-done((f32[2,2,32,128]{3,2,1,0:T(8,128)S(1)}, f32[2,2,32,128]{3,2,1,0:T(8,128)S(1)}, u32[]{:S(2)}, u32[]{:S(2)}) %collective-permute-start) | collective-permute-done | bytes 65568 | tf_op jit(solution)/shard_map/ppermute | solution.py:492
  8.5 0.6 copy-done.4
  9.1 1.8 %shard_map.92 = (f32[32,2,32,128]{3,2,1,0:T(8,128)}, f32[40,256]{1,0:T(8,128)}) custom-call(f32[2,2,32,128]{3,2,1,0:T(8,128)} %copy-done.4, f32[3,2,32,128]{3,2,1,0:T(8,128)} %get-tuple-element.19.edge_ref, s32[8,256]{1,0:T(8,128)} %get-tuple-element.20.cell_ref, f32[40,256]{1,0:T(8,128)} %get-tuple-element.21.partial_ref, ...), custom_call_target="tpu_custom_call", output_to_operand_aliasing={{0}: (4, {})} | custom-call | flops 10000000 | bytes 1000000 | tf_op jit(solution)/shard_map/pallas_call | solution.py:453
  11.0 23.5 %all_gather.3 = f32[640,256]{1,0:T(8,128)S(1)} all-gather(f32[40,256]{1,0:T(8,128)} %get-tuple-element.23), channel_id=1, replica_groups=mesh['mem'=16,'tile'=16] {'mem'}, dimensions={0}, use_global_device_ids=true | all-gather | bytes 696320 | tf_op jit(solution)/shard_map/all_gather | solution.py:520
  34.5 1.6 %collective-permute-start.1 = (f32[640,256]{1,0:T(8,128)S(1)}, f32[640,256]{1,0:T(8,128)S(1)}, u32[]{:S(2)}, u32[]{:S(2)}) collective-permute-start(f32[640,256]{1,0:T(8,128)S(1)} %all_gather.3), channel_id=1, source_target_pairs={{0,1},{1,2},{2,3},{3,4},{4,5},{5,6},{6,7},{7,8},{8,9},{9,10},{10,1... | collective-permute-start | bytes 1966088 | tf_op jit(solution)/shard_map/ppermute | solution.py:502
  36.1 3.8 %all-to-all-start = ((f32[16,2,2,32,128]{4,3,2,1,0:T(8,128)}), f32[16,2,2,32,128]{4,3,2,1,0:T(8,128)S(1)}, u32[]{:S(2)}, u32[]{:S(2)}) async-start(f32[16,2,2,32,128]{4,3,2,1,0:T(8,128)} %bitcast.15), calls=%async_computation | async-start | bytes 2097152 | tf_op jit(solution)/shard_map/all_to_all | solution.py:525
  39.8 4.4 %collective-permute-done.1 = f32[640,256]{1,0:T(8,128)S(1)} collective-permute-done((f32[640,256]{1,0:T(8,128)S(1)}, f32[640,256]{1,0:T(8,128)S(1)}, u32[]{:S(2)}, u32[]{:S(2)}) %collective-permute-start.1) | collective-permute-done | bytes 655392 | tf_op jit(solution)/shard_map/ppermute | solution.py:502
  44.2 4.3 %collective-permute-start.2 = (f32[640,256]{1,0:T(8,128)S(1)}, f32[640,256]{1,0:T(8,128)S(1)}, u32[]{:S(2)}, u32[]{:S(2)}) collective-permute-start(f32[640,256]{1,0:T(8,128)S(1)} %collective-permute-done.1), channel_id=1, source_target_pairs={{0,16},{16,0},{32,48},{48,32},{64,80},{80,64},{96,112},{112,96},{1... | collective-permute-start | bytes 1966088 | tf_op jit(solution)/shard_map/ppermute | solution.py:503
  48.5 0.8 copy-done.2
  49.4 0.0 copy-done.5
  49.4 0.0 copy-done.7
  49.4 0.1 select_reduce_fusion.1
  49.5 0.0 copy-done.6
  49.5 0.0 copy-done.8
  49.5 0.1 compare_select_fusion.2
  49.6 0.4 select_reduce_fusion.wsum_ref
  50.0 0.3 collective-permute-done.2
  50.3 0.0 copy-done
  50.3 1.1 copy-done.1
  51.3 1.1 copy-done.3
  52.4 24.1 %shard_map.93 = (f32[2,512,512]{2,1,0:T(8,128)S(1)}, f32[2,8,512]{2,1,0:T(8,128)S(1)}) custom-call(f32[16,40,256]{2,1,0:T(8,128)S(1)} %bitcast.13, f32[16,40,256]{2,1,0:T(8,128)S(1)} %bitcast.12, f32[16,40,256]{2,1,0:T(8,128)S(1)} %bitcast.14, f32[2,768]{1,0:T(2,128)S(1)} %select_reduce_fusion.wsum_ref), custom_call_target="tpu_custom_call" | custom-call | flops 24999999488 | bytes 4000000 | tf_op jit(solution)/shard_map/pallas_call | solution.py:279
  76.5 0.0 all-to-all-done.cols_ref
  76.5 1.2 %shard_map.94 = f32[16,2,2,32,128]{4,3,2,1,0:T(8,128)S(1)} custom-call(f32[2,512,512]{2,1,0:T(8,128)S(1)} %get-tuple-element.30.root_ref, f32[2,8,512]{2,1,0:T(8,128)S(1)} %get-tuple-element.31.rhs_ref, f32[16,2,2,32,128]{4,3,2,1,0:T(8,128)S(1)} %all-to-all-done.cols_ref), custom_call_target="tpu_custom_call" | custom-call | flops 800000000 | bytes 4000000 | tf_op jit(solution)/shard_map/pallas_call | solution.py:323
  77.7 33.7 %all_to_all.10.part_ref = f32[16,2,2,32,128]{4,3,2,1,0:T(8,128)S(1)} all-to-all(f32[16,2,2,32,128]{4,3,2,1,0:T(8,128)S(1)} %shard_map.94), channel_id=1, replica_groups=mesh['mem'=16,'tile'=16] {'mem'}, dimensions={0} | all-to-all | bytes 2097152 | tf_op jit(solution)/shard_map/all_to_all | solution.py:544
  111.4 2.0 %shard_map.95 = f32[2048,128]{1,0:T(8,128)} custom-call(f32[16,2,2,32,128]{4,3,2,1,0:T(8,128)S(1)} %all_to_all.10.part_ref), custom_call_target="tpu_custom_call" | custom-call | tf_op jit(solution)/shard_map/pallas_call | solution.py:481
  (7 shorter events, 0.0 us)
Async XLA Ops:
  1.0 7.5 %collective-permute-start = (f32[2,2,32,128]{3,2,1,0:T(8,128)S(1)}, f32[2,2,32,128]{3,2,1,0:T(8,128)S(1)}, u32[]{:S(2)}, u32[]{:S(2)}) collective-permute-start(f32[2,2,32,128]{3,2,1,0:T(8,128)S(1)} %bitcast.17), channel_id=1, source_target_pairs={{0,1},{1,2},{2,3},{3,4},{4,5},{5,6},{6,7},{7,8},{8,9},{9,10},{10,1... | collective-permute-start | bytes 196616 | tf_op jit(solution)/shard_map/ppermute | solution.py:492
  7.1 42.3 %copy-start.5 = (s32[2,512]{1,0:T(2,128)S(1)}, s32[2,512]{1,0:T(2,128)}, u32[]{:S(2)}) copy-start(s32[2,512]{1,0:T(2,128)} %param.15) | copy-start | bytes 12292
  7.1 42.3 %copy-start.7 = (f32[16]{0:T(128)S(1)}, f32[16]{0:T(128)}, u32[]{:S(2)}) copy-start(f32[16]{0:T(128)} %param.17) | copy-start | bytes 196
  7.1 42.3 %copy-start.6 = (s32[2,512]{1,0:T(2,128)S(1)}, s32[2,512]{1,0:T(2,128)}, u32[]{:S(2)}) copy-start(s32[2,512]{1,0:T(2,128)} %param.14) | copy-start | bytes 12292
  7.1 42.4 %copy-start.8 = (s32[2]{0:T(128)S(1)}, s32[2]{0:T(128)}, u32[]{:S(2)}) copy-start(s32[2]{0:T(128)} %param.16) | copy-start | bytes 28
  8.5 0.6 copy-start.4
  34.5 15.8 %copy-start = (f32[640,256]{1,0:T(8,128)}, f32[640,256]{1,0:T(8,128)S(1)}, u32[]{:S(2)}) copy-start(f32[640,256]{1,0:T(8,128)S(1)} %all_gather.3) | copy-start | bytes 1966084
  34.5 9.7 %collective-permute-start.1 = (f32[640,256]{1,0:T(8,128)S(1)}, f32[640,256]{1,0:T(8,128)S(1)}, u32[]{:S(2)}, u32[]{:S(2)}) collective-permute-start(f32[640,256]{1,0:T(8,128)S(1)} %all_gather.3), channel_id=1, source_target_pairs={{0,1},{1,2},{2,3},{3,4},{4,5},{5,6},{6,7},{7,8},{8,9},{9,10},{10,1... | collective-permute-start | bytes 1966088 | tf_op jit(solution)/shard_map/ppermute | solution.py:502
  36.1 40.5 %all-to-all-start = ((f32[16,2,2,32,128]{4,3,2,1,0:T(8,128)}), f32[16,2,2,32,128]{4,3,2,1,0:T(8,128)S(1)}, u32[]{:S(2)}, u32[]{:S(2)}) async-start(f32[16,2,2,32,128]{4,3,2,1,0:T(8,128)} %bitcast.15), calls=%async_computation | async-start | bytes 2097152 | tf_op jit(solution)/shard_map/all_to_all | solution.py:525
  44.2 6.1 %collective-permute-start.2 = (f32[640,256]{1,0:T(8,128)S(1)}, f32[640,256]{1,0:T(8,128)S(1)}, u32[]{:S(2)}, u32[]{:S(2)}) collective-permute-start(f32[640,256]{1,0:T(8,128)S(1)} %collective-permute-done.1), channel_id=1, source_target_pairs={{0,16},{16,0},{32,48},{48,32},{64,80},{80,64},{96,112},{112,96},{1... | collective-permute-start | bytes 1966088 | tf_op jit(solution)/shard_map/ppermute | solution.py:503
  48.5 0.8 copy-start.2
  50.3 1.1 copy-start.1
  51.3 1.1 copy-start.3
where the time goes:
time: 114 us; the launch traced here: 113 us
  blocking collectives  57.2 us (50%)
  Pallas kernels  33 us (29%)
  starting transfers between devices  11.9 us (10%)
  waiting for transfers between devices  5.96 us (5%)
  local copies, waits for them, and re-layouts  4.66 us (4%)
    all_to_all x1, blocking collectives, on_device(): return restore(lax.all_to_all(parts, 'mem', 0, 0, tiled=True))  33.7 us
    pallas_call x1, Pallas kernels, inverse_roots(): pl.pallas_call(root_kernel, out_shape=(jax.ShapeDtypeStruct(square, F32),...  24.1 us
    all_gather x1, blocking collectives, on_device(): own = lax.all_gather(message, 'mem', axis=0, tiled=True)  23.5 us
    ppermute x1, waiting for transfers between devices, neighbours(): near = lax.ppermute(value, ('mem', 'tile'), pairs)  4.36 us
    ppermute x1, starting transfers between devices, neighbours(): far = lax.ppermute(near, 'mem', [(m, m ^ 1) for m in range(mem)])  4.34 us
    pallas_call x1, Pallas kernels, inner_forecast(): pl.pallas_call(inner_kernel, out_shape=(jax.ShapeDtypeStruct((lines, leve...  3.9 us
    all_to_all x1, starting transfers between devices, on_device(): lax.all_to_all(field.reshape(devices, lines // devices, levels, mem_dev,...  3.76 us
    unnamed x19, local copies, waits for them, and re-layouts  3.68 us
  transfers between devices with their start and end apart: 4, of which 3 were waited for; matrix products, arithmetic and copies ran while one was open for 1% of the time, Pallas kernels for 25%

commit v1 on v0

--- a/solution.py
+++ b/solution.py
@@ -12,7 +12,8 @@
 HALF = 256
 PAD = 16
 NARROW = 32.0
-SMALL, MID, LOW = 1.0 / 5, 1.0 / 32, 1.0 / 1024
+SMALL = (1.0 / 5, 1.0 / 16, 1.0 / 64)
+MID, LOW = 1.0 / 4, 1.0 / 32
 BF = jnp.bfloat16
 F32 = jnp.float32
 LO, HI = slice(0, HALF), slice(HALF, 2 * HALF)
@@ -31,12 +32,70 @@
     return lax.dot_general(left, right, (((1,), (1,)), ((), ())), preferred_element_type=F32)
 
 
-def root_kernel(near_ref, own_ref, far_ref, wsum_ref, out_ref, rhs_ref, bh, bl, t, p, ph, pl_, gh, gl, z, zh, zl):
-    devices, _, obs_tile = own_ref.shape
+def add_part(n, spot, block_ref, wsum_ref, bh, bl, old, old_rhs, new, new_rhs):
+    devices, rows, obs_tile = block_ref.shape
+    members = bl.shape[1]
+    mem_dev = members // devices
+    top = 2 * PAD
+    block = block_ref[:, 0:mem_dev, :].reshape(members, obs_tile)
+    mean = jnp.sum(block, axis=0, keepdims=True) * (1.0 / members)
+    value = block_ref[0, mem_dev : mem_dev + 1, :]
+    total = block_ref[0, mem_dev + 1 : mem_dev + 2, :] * wsum_ref[n : n + 1, spot]
+    root = jnp.where(total > 0.0, jnp.sqrt(jnp.maximum(total, 1e-30)), 0.0)
+    row = jnp.broadcast_to(root * (value - mean), (PAD, obs_tile))
+    bh[n, 0:PAD, :], bh[n, PAD:top, :] = split(row)
+    bh[n, top:, :], bl[n] = split((block - mean) * root)
+    first = bh[n, 0 : top + HALF, :]
+    second = bh[n, top + HALF :, :]
+    left = mm_t(first, first[top:, :])
+    right = mm_t(first, second)
+    left_low = mm_t(first, bl[n, LO, :])
+    right_low = mm_t(first, bl[n, HI, :])
+    sums = {
+        (0, 0): 0.5 * left[top:] + left_low[top:],
+        (0, 1): right[top:] + right_low[top:],
+        (1, 0): mm_t(second, bl[n, LO, :]),
+        (1, 1): 0.5 * mm_t(second, second) + mm_t(second, bl[n, HI, :]),
+    }
+    for (a, b), value in sums.items():
+        spot_a, spot_b = (LO, HI)[a], (LO, HI)[b]
+        new[n, spot_a, spot_b] = value if old is None else value + old[n, spot_a, spot_b]
+    for spot_b, high, low in ((LO, left, left_low), (HI, right, right_low)):
+        rhs = jnp.broadcast_to(high[0:1] + high[PAD : PAD + 1] + low[0:1], (8, HALF))
+        new_rhs[n, :, spot_b] = rhs if old_rhs is None else rhs + old_rhs[n, :, spot_b]
+
+
+def part_kernel(spot, block_ref, wsum_ref, *refs):
+    old, old_rhs = refs[:-4] if len(refs) == 6 else (None, None)
+    new, new_rhs, bh, bl = refs[-4:]
+    for n in range(new.shape[0]):
+        add_part(n, spot, block_ref, wsum_ref, bh, bl, old, old_rhs, new, new_rhs)
+
+
+def gram_part(which, block, wsum, members, sofar=()):
+    patches, obs_tile = wsum.shape[0], block.shape[2]
+    spot = slice(which * obs_tile, (which + 1) * obs_tile)
+    return pl.pallas_call(
+        functools.partial(part_kernel, spot),
+        out_shape=(
+            jax.ShapeDtypeStruct((patches, members, members), F32),
+            jax.ShapeDtypeStruct((patches, 8, members), F32),
+        ),
+        scratch_shapes=[
+            pltpu.VMEM((patches, 2 * PAD + members, obs_tile), BF),
+            pltpu.VMEM((patches, members, obs_tile), BF),
+        ],
+        compiler_params=pltpu.CompilerParams(vmem_limit_bytes=24 * 1024 * 1024),
+        cost_estimate=pl.CostEstimate(flops=2 * 10**9, bytes_accessed=4 * 10**6, transcendentals=0),
+    )(block, wsum, *sofar)
+
+
+def root_kernel(
+    far_ref, wsum_ref, gram_ref, part_ref, out_ref, rhs_ref, bh, bl, t, p, ph, pl_, gh, gl, z, zh, zl
+):
+    devices, _, obs_tile = far_ref.shape
     patches, members = out_ref.shape[:2]
-    mem_dev = members // devices
     inv = 1.0 / (members - 1)
-    top = 2 * PAD
     eye = (
         lax.broadcasted_iota(jnp.int32, (HALF, HALF), 0)
         == lax.broadcasted_iota(jnp.int32, (HALF, HALF), 1)
@@ -48,30 +107,9 @@
         high[n, rows, cols], low[n, rows, cols] = split(value)
 
     def gram(n):
-        for j, ref in enumerate((near_ref, own_ref, far_ref)):
-            spot = slice(j * obs_tile, (j + 1) * obs_tile)
-            block = ref[:, 0:mem_dev, :].reshape(members, obs_tile)
-            mean = jnp.sum(block, axis=0, keepdims=True) * (1.0 / members)
-            value = ref[0, mem_dev : mem_dev + 1, :]
-            total = ref[0, mem_dev + 1 : mem_dev + 2, :] * wsum_ref[n : n + 1, spot]
-            root = jnp.where(total > 0.0, jnp.sqrt(jnp.maximum(total, 1e-30)), 0.0)
-            row = jnp.broadcast_to(root * (value - mean), (PAD, obs_tile))
-            bh[n, 0:PAD, spot], bh[n, PAD:top, spot] = split(row)
-            bh[n, top:, spot], bl[n, :, spot] = split((block - mean) * root)
-        first = bh[n, 0 : top + HALF, :]
-        second = bh[n, top + HALF :, :]
-        left = mm_t(first, first[top:, :])
-        right = mm_t(first, second)
-        left_low = mm_t(first, bl[n, LO, :])
-        right_low = mm_t(first, bl[n, HI, :])
-        t[n, LO, LO] = 0.5 * left[top:] + left_low[top:]
-        t[n, LO, HI] = right[top:] + right_low[top:]
-        rhs0 = (left[0:1] + left[PAD : PAD + 1] + left_low[0:1]) * inv
-        rhs1 = (right[0:1] + right[PAD : PAD + 1] + right_low[0:1]) * inv
-        rhs_ref[n, :, LO] = jnp.broadcast_to(rhs0, (8, HALF))
-        rhs_ref[n, :, HI] = jnp.broadcast_to(rhs1, (8, HALF))
-        t[n, HI, LO] = mm_t(second, bl[n, LO, :])
-        t[n, HI, HI] = 0.5 * mm_t(second, second) + mm_t(second, bl[n, HI, :])
+        spot = slice(2 * obs_tile, 3 * obs_tile)
+        add_part(n, spot, far_ref, wsum_ref, bh, bl, gram_ref, part_ref, t, rhs_ref)
+        rhs_ref[n] = rhs_ref[n] * inv
 
     def start(n):
         g00 = (t[n, LO, LO] + t[n, LO, LO].T) * inv + eye
@@ -123,6 +161,18 @@
         z11 = 1.5 * z[n, HI, HI] - 0.5 * product(n, zh, zl, HI, HI)
         return z00, z10, z11
 
+    def few_factor(n, lead):
+        gl[n, LO, LO] = (z[n, LO, LO] - lead * eye).astype(BF)
+        gl[n, HI, LO] = z[n, HI, LO].astype(BF)
+        gl[n, LO, HI] = z[n, HI, LO].T.astype(BF)
+        gl[n, HI, HI] = (z[n, HI, HI] - lead * eye).astype(BF)
+
+        def moved(rows, cols):
+            part = lead * p[n, rows, cols] + mm(ph[n, rows, :], gl[n, :, cols])
+            return 1.5 * z[n, rows, cols] - 0.5 * part
+
+        return moved(LO, LO), moved(HI, LO), moved(HI, HI)
+
     def keep(n, parts):
         z00, z10, z11 = parts
         put(z00, z, zh, zl, n, LO, LO)
@@ -144,18 +194,9 @@
         put(n10.T, None, ph, pl_, n, LO, HI)
         put(n11, p, ph, pl_, n, HI, HI)
 
-    def sizes(n):
+    def mean_square(n):
         p00, p10, p11 = p[n, LO, LO], p[n, HI, LO], p[n, HI, HI]
-        total = jnp.sum(p00 * p00 + 2.0 * (p10 * p10) + p11 * p11) * (1.0 / members)
-        trace = jnp.sum((p00 + p11) * eye) * (1.0 / members)
-        return total, 1.0 - 2.0 * trace + total
-
-    def widest():
-        small, near = sizes(0)
-        for n in range(1, patches):
-            other_small, other_near = sizes(n)
-            small, near = jnp.maximum(small, other_small), jnp.maximum(near, other_near)
-        return small, near
+        return jnp.sum(p00 * p00 + 2.0 * (p10 * p10) + p11 * p11) * (1.0 / members)
 
     def near_one(n):
         e10 = -p[n, HI, LO]
@@ -195,12 +236,14 @@
         gram(n)
     scales = [start(n) for n in every]
 
-    def sweep(first, one_pass):
+    def sweep(lead, one_pass):
         for n in every:
             square(n)
         for n in every:
+            if one_pass and lead is not None:
+                keep(n, few_factor(n, lead))
             squared(n, one_pass)
-            if not first:
+            if not one_pass and lead is not None:
                 keep(n, factor(n))
             cube(n, one_pass)
 
@@ -214,45 +257,49 @@
             keep(n, near_factor(n) if one_pass else factor(n))
             near_cube(n)
 
-    spread = jnp.max(jnp.concatenate(scales, 0))
-    narrow = spread <= NARROW
-    small, _ = widest()
-
-    few = jnp.logical_and(small <= SMALL, narrow)
-
-    @pl.when(jnp.logical_not(few))
+    least = jnp.min(1.0 / jnp.concatenate(scales, 0))
+    mean = mean_square(0)
+    for n in range(1, patches):
+        mean = jnp.maximum(mean, mean_square(n))
+    count = sum((mean <= bound).astype(jnp.int32) for bound in SMALL)
+    count = jnp.where(least >= 1.0 / NARROW, count, 0)
+
+    def onward(value):
+        return 0.25 * value * (3.0 - value) * (3.0 - value)
+
+    @pl.when(count == 0)
     def _():
-        sweep(True, False)
-
-    @pl.when(few)
+        sweep(None, False)
+
+    @pl.when(count > 0)
     def _():
-        sweep(True, True)
-
-    def step(_, carry):
-        small, near = carry
-
-        few = jnp.logical_and(small <= SMALL, narrow)
+        sweep(None, True)
+
+    def step(k, carry):
+        least, lead = carry
+        few = k < count
         rest = jnp.logical_not(few)
+        wide = 1.0 - least
 
         @pl.when(few)
         def _():
-            sweep(False, True)
-
-        @pl.when(jnp.logical_and(rest, near > MID))
+            sweep(lead, True)
+
+        @pl.when(jnp.logical_and(rest, wide > MID))
         def _():
-            sweep(False, False)
-
-        @pl.when(jnp.logical_and(rest, jnp.logical_and(near <= MID, near > LOW)))
+            sweep(lead, False)
+
+        @pl.when(jnp.logical_and(rest, jnp.logical_and(wide <= MID, wide > LOW)))
         def _():
             near_sweep(False)
 
-        @pl.when(jnp.logical_and(rest, near <= LOW))
+        @pl.when(jnp.logical_and(rest, wide <= LOW))
         def _():
             near_sweep(True)
 
-        return widest()
-
-    _, near = lax.fori_loop(0, NS_ITERS - 2, step, widest())
+        return onward(least), 1.5 * lead
+
+    least, _ = lax.fori_loop(1, NS_ITERS - 1, step, (onward(least), jnp.float32(1.5)))
 
     def finish(make):
         for n in every:
@@ -262,11 +309,11 @@
             out_ref[n, LO, HI] = z10.T * lax.rsqrt(scales[n])
             out_ref[n, HI, HI] = z11 * lax.rsqrt(scales[n])
 
-    @pl.when(near > LOW)
+    @pl.when(1.0 - least > LOW)
     def _():
         finish(factor)
 
-    @pl.when(near <= LOW)
+    @pl.when(1.0 - least <= LOW)
     def _():
         for n in every:
             near_one(n)
@@ -274,7 +321,9 @@
 
 
 def inverse_roots(near, own, far, wsum, members):
-    patches, nobs = wsum.shape
+    sofar = gram_part(1, own, wsum, members)
+    sofar = gram_part(0, near, wsum, members, sofar)
+    patches, obs_tile = wsum.shape[0], far.shape[2]
     square = (patches, members, members)
     return pl.pallas_call(
         root_kernel,
@@ -283,8 +332,8 @@
             jax.ShapeDtypeStruct((patches, 8, members), F32),
         ),
         scratch_shapes=[
-            pltpu.VMEM((patches, 2 * PAD + members, nobs), BF),
-            pltpu.VMEM((patches, members, nobs), BF),
+            pltpu.VMEM((patches, 2 * PAD + members, obs_tile), BF),
+            pltpu.VMEM((patches, members, obs_tile), BF),
             pltpu.VMEM(square, F32),
             pltpu.VMEM(square, F32),
             pltpu.VMEM(square, BF),
@@ -297,7 +346,7 @@
         ],
         compiler_params=pltpu.CompilerParams(vmem_limit_bytes=28 * 1024 * 1024),
         cost_estimate=pl.CostEstimate(flops=25 * 10**9, bytes_accessed=4 * 10**6, transcendentals=0),
-    )(near, own, far, wsum)
+    )(far, wsum, *sofar)
 
 
 def apply_kernel(root_ref, rhs_ref, cols_ref, out_ref):
@@ -465,14 +514,23 @@
     )(*small, field)
 
 
-def restore_kernel(part_ref, out_ref):
+def restore_kernel(part_ref, out_hbm, out_ref, sems):
     devices, patches, levels, mem_dev, nlat = part_ref.shape
     lines = patches * devices
-    for device in range(devices):
-        for n in range(patches):
-            for lev in range(levels):
-                rows = pl.ds(lev * lines + patches * device + n, mem_dev, stride=levels * lines)
-                out_ref[rows, :] = part_ref[device, n, lev]
+    group = 8
+    copies = []
+    for i in range(mem_dev // group):
+        for device in range(devices):
+            for n in range(patches):
+                for lev in range(levels):
+                    first = i * group * levels * lines + lev * lines + patches * device + n
+                    rows = pl.ds(first, group, stride=levels * lines)
+                    out_ref[rows, :] = part_ref[device, n, lev, i * group : (i + 1) * group, :]
+        spot = pl.ds(i * group * levels * lines, group * levels * lines)
+        copies.append(pltpu.make_async_copy(out_ref.at[spot], out_hbm.at[spot], sems.at[i]))
+        copies[-1].start()
+    for copy in copies:
+        copy.wait()
 
 
 def restore(parts):
@@ -481,6 +539,12 @@
     out = pl.pallas_call(
         restore_kernel,
         out_shape=jax.ShapeDtypeStruct((rows, nlat), F32),
+        in_specs=[pl.BlockSpec(memory_space=pltpu.VMEM)],
+        out_specs=pl.BlockSpec(memory_space=pl.ANY),
+        scratch_shapes=[
+            pltpu.VMEM((rows, nlat), F32),
+            pltpu.SemaphoreType.DMA((mem_dev // 8,)),
+        ],
         compiler_params=pltpu.CompilerParams(vmem_limit_bytes=24 * 1024 * 1024),
     )(parts)
     return out.reshape(mem_dev, levels, patches * devices, nlat)

time: 114 us -> 108 us (0.947)
  local copies, waits for them, and re-layouts: 4.66 us -> 1.63 us
  blocking collectives: 57.2 us -> 55.6 us
  Pallas kernels: 33 us -> 31.6 us
    unnamed x19 -> x11, local copies, waits for them, and re-layouts: 3.68 us -> 0.65 us
    pallas_call x1, Pallas kernels: 24.1 us -> 21.4 us  [inverse_roots(): pl.pallas_call(root_kernel, out_shape=(jax.ShapeDtypeStruct(square, F32),...]
    pallas_call x0 -> x2, Pallas kernels: none -> 1.68 us  [gram_part(): pl.pallas_call(functools.partial(part_kernel, spot), out_shape=(jax.Shape...]
    all_to_all x1, blocking collectives: 33.7 us -> 32.1 us  [on_device(): return restore(lax.all_to_all(parts, 'mem', 0, 0, tiled=True))]
  transfers between devices with their start and end apart: 4 -> 4, of which waited for: 3 -> 2; matrix products, arithmetic and copies ran while one was open for 1% -> 1% of each run, Pallas kernels for 25% -> 25%
where the time goes in v1:
time: 108 us; the launch traced here: 107 us
  blocking collectives  55.6 us (51%)
  Pallas kernels  31.6 us (29%)
  starting transfers between devices  11.9 us (11%)
  waiting for transfers between devices  5.51 us (5%)
  local copies, waits for them, and re-layouts  1.63 us (2%)
    all_to_all x1, blocking collectives, on_device(): return restore(lax.all_to_all(parts, 'mem', 0, 0, tiled=True))  32.1 us
    all_gather x1, blocking collectives, on_device(): own = lax.all_gather(message, 'mem', axis=0, tiled=True)  23.5 us
    pallas_call x1, Pallas kernels, inverse_roots(): pl.pallas_call(root_kernel, out_shape=(jax.ShapeDtypeStruct(square, F32),...  21.4 us
    ppermute x1, starting transfers between devices, neighbours(): far = lax.ppermute(near, 'mem', [(m, m ^ 1) for m in range(mem)])  4.34 us
    ppermute x1, waiting for transfers between devices, neighbours(): near = lax.ppermute(value, ('mem', 'tile'), pairs)  4.18 us
    pallas_call x1, Pallas kernels, inner_forecast(): pl.pallas_call(inner_kernel, out_shape=(jax.ShapeDtypeStruct((lines, leve...  3.9 us
    all_to_all x1, starting transfers between devices, on_device(): lax.all_to_all(field.reshape(devices, lines // devices, levels, mem_dev,...  3.76 us
    ppermute x1, starting transfers between devices, shifted(): return lax.ppermute(value, axis, pairs)  2.2 us
  transfers between devices with their start and end apart: 4, of which 2 were waited for; matrix products, arithmetic and copies ran while one was open for 1% of the time, Pallas kernels for 25%

profile of v1, /device:TPU:1, one launch (start us, length us, event | category | flops | bytes accessed | tf_op | source)
XLA Modules:
  0.0 107.1 jit_solution(172555097861741080)
XLA Ops:
  0.0 1.0 slice.3
  1.0 2.2 %collective-permute-start = (f32[2,2,32,128]{3,2,1,0:T(8,128)S(1)}, f32[2,2,32,128]{3,2,1,0:T(8,128)S(1)}, u32[]{:S(2)}, u32[]{:S(2)}) collective-permute-start(f32[2,2,32,128]{3,2,1,0:T(8,128)S(1)} %bitcast.17), channel_id=1, source_target_pairs={{0,1},{1,2},{2,3},{3,4},{4,5},{5,6},{6,7},{7,8},{8,9},{9,10},{10,1... | collective-permute-start | bytes 196616 | tf_op jit(solution)/shard_map/ppermute | solution.py:556
  3.2 3.9 %shard_map.91 = (f32[32,2,32,128]{3,2,1,0:T(8,128)}, f32[3,2,32,128]{3,2,1,0:T(8,128)}, f32[40,256]{1,0:T(8,128)}, s32[8,256]{1,0:T(8,128)}) custom-call(f32[2048,128]{1,0:T(8,128)} %bitcast.16, f32[2,128]{1,0:T(2,128)} %courant_hbm.1, s32[1,256]{1,0:T(1,128)} %bitcast.18, f32[1,256]{1,0:T(1,128)} %bitcast.19, f32[1,256]{1,0:T(1,128)} %bitcast.20), custom_call_target="tpu_custom_call" | custom-call | flops 100000000 | bytes 2000000 | tf_op jit(solution)/shard_map/pallas_call | solution.py:449
  7.1 0.0 copy-start.1
  7.1 0.0 copy-start.3
  7.1 0.0 copy-start.4
  7.1 0.0 copy-start.2
  7.2 1.3 %collective-permute-done.halo_ref = f32[2,2,32,128]{3,2,1,0:T(8,128)S(1)} collective-permute-done((f32[2,2,32,128]{3,2,1,0:T(8,128)S(1)}, f32[2,2,32,128]{3,2,1,0:T(8,128)S(1)}, u32[]{:S(2)}, u32[]{:S(2)}) %collective-permute-start) | collective-permute-done | bytes 65568 | tf_op jit(solution)/shard_map/ppermute | solution.py:556
  8.5 0.0 copy-start
  8.5 0.6 copy-done
  9.1 1.8 %shard_map.92 = (f32[32,2,32,128]{3,2,1,0:T(8,128)}, f32[40,256]{1,0:T(8,128)}) custom-call(f32[2,2,32,128]{3,2,1,0:T(8,128)} %copy-done, f32[3,2,32,128]{3,2,1,0:T(8,128)} %get-tuple-element.23.edge_ref, s32[8,256]{1,0:T(8,128)} %get-tuple-element.24.cell_ref, f32[40,256]{1,0:T(8,128)} %get-tuple-element.25.partial_ref, ...), custom_call_target="tpu_custom_call", output_to_operand_aliasing={{0}: (4, {})} | custom-call | flops 10000000 | bytes 1000000 | tf_op jit(solution)/shard_map/pallas_call | solution.py:502
  10.9 23.5 %all_gather.3 = f32[640,256]{1,0:T(8,128)S(1)} all-gather(f32[40,256]{1,0:T(8,128)} %get-tuple-element.27), channel_id=1, replica_groups=mesh['mem'=16,'tile'=16] {'mem'}, dimensions={0}, use_global_device_ids=true | all-gather | bytes 696320 | tf_op jit(solution)/shard_map/all_gather | solution.py:584
  34.4 1.6 %collective-permute-start.1 = (f32[640,256]{1,0:T(8,128)S(1)}, f32[640,256]{1,0:T(8,128)S(1)}, u32[]{:S(2)}, u32[]{:S(2)}) collective-permute-start(f32[640,256]{1,0:T(8,128)S(1)} %all_gather.3), channel_id=1, source_target_pairs={{0,1},{1,2},{2,3},{3,4},{4,5},{5,6},{6,7},{7,8},{8,9},{9,10},{10,1... | collective-permute-start | bytes 1966088 | tf_op jit(solution)/shard_map/ppermute | solution.py:566
  36.0 3.8 %all-to-all-start = ((f32[16,2,2,32,128]{4,3,2,1,0:T(8,128)}), f32[16,2,2,32,128]{4,3,2,1,0:T(8,128)S(1)}, u32[]{:S(2)}, u32[]{:S(2)}) async-start(f32[16,2,2,32,128]{4,3,2,1,0:T(8,128)} %bitcast.15), calls=%async_computation | async-start | bytes 2097152 | tf_op jit(solution)/shard_map/all_to_all | solution.py:589
  39.8 0.0 copy-done.1
  39.8 0.0 copy-done.3
  39.8 0.1 select_reduce_fusion.1
  39.9 0.0 copy-done.4
  39.9 0.1 compare_select_fusion.2
  40.0 4.2 %collective-permute-done.1 = f32[640,256]{1,0:T(8,128)S(1)} collective-permute-done((f32[640,256]{1,0:T(8,128)S(1)}, f32[640,256]{1,0:T(8,128)S(1)}, u32[]{:S(2)}, u32[]{:S(2)}) %collective-permute-start.1) | collective-permute-done | bytes 655392 | tf_op jit(solution)/shard_map/ppermute | solution.py:566
  44.2 4.3 %collective-permute-start.2 = (f32[640,256]{1,0:T(8,128)S(1)}, f32[640,256]{1,0:T(8,128)S(1)}, u32[]{:S(2)}, u32[]{:S(2)}) collective-permute-start(f32[640,256]{1,0:T(8,128)S(1)} %collective-permute-done.1), channel_id=1, source_target_pairs={{0,16},{16,0},{32,48},{48,32},{64,80},{80,64},{96,112},{112,96},{1... | collective-permute-start | bytes 1966088 | tf_op jit(solution)/shard_map/ppermute | solution.py:567
  48.5 0.0 copy-done.2
  48.5 0.4 select_reduce_fusion.wsum_ref
  48.9 0.8 shard_map.93
  49.8 0.9 shard_map.94
  50.6 0.0 collective-permute-done.2
  50.6 21.4 %shard_map.95 = (f32[2,512,512]{2,1,0:T(8,128)S(1)}, f32[2,8,512]{2,1,0:T(8,128)S(1)}) custom-call(f32[16,40,256]{2,1,0:T(8,128)S(1)} %bitcast.14, f32[2,768]{1,0:T(2,128)S(1)} %select_reduce_fusion.wsum_ref, f32[2,512,512]{2,1,0:T(8,128)S(1)} %get-tuple-element.36.gram_ref, f32[2,8,512]{2,1,0:T(8,128)S(1)} %get-tuple-element.37.part_ref), custom_call_target="tpu_custom_call" | custom-call | flops 24999999488 | bytes 4000000 | tf_op jit(solution)/shard_map/pallas_call | solution.py:328
  72.1 0.0 all-to-all-done.cols_ref
  72.1 1.2 %shard_map.96 = f32[16,2,2,32,128]{4,3,2,1,0:T(8,128)S(1)} custom-call(f32[2,512,512]{2,1,0:T(8,128)S(1)} %get-tuple-element.38.root_ref, f32[2,8,512]{2,1,0:T(8,128)S(1)} %get-tuple-element.39.rhs_ref, f32[16,2,2,32,128]{4,3,2,1,0:T(8,128)S(1)} %all-to-all-done.cols_ref), custom_call_target="tpu_custom_call" | custom-call | flops 800000000 | bytes 4000000 | tf_op jit(solution)/shard_map/pallas_call | solution.py:372
  73.3 32.1 %all_to_all.10.part_ref = f32[16,2,2,32,128]{4,3,2,1,0:T(8,128)S(1)} all-to-all(f32[16,2,2,32,128]{4,3,2,1,0:T(8,128)S(1)} %shard_map.96), channel_id=1, replica_groups=mesh['mem'=16,'tile'=16] {'mem'}, dimensions={0} | all-to-all | bytes 2097152 | tf_op jit(solution)/shard_map/all_to_all | solution.py:608
  105.4 1.6 %shard_map.97 = f32[2048,128]{1,0:T(8,128)} custom-call(f32[16,2,2,32,128]{4,3,2,1,0:T(8,128)S(1)} %all_to_all.10.part_ref), custom_call_target="tpu_custom_call" | custom-call | tf_op jit(solution)/shard_map/pallas_call | solution.py:539
  (2 shorter events, 0.0 us)
Async XLA Ops:
  1.0 7.5 %collective-permute-start = (f32[2,2,32,128]{3,2,1,0:T(8,128)S(1)}, f32[2,2,32,128]{3,2,1,0:T(8,128)S(1)}, u32[]{:S(2)}, u32[]{:S(2)}) collective-permute-start(f32[2,2,32,128]{3,2,1,0:T(8,128)S(1)} %bitcast.17), channel_id=1, source_target_pairs={{0,1},{1,2},{2,3},{3,4},{4,5},{5,6},{6,7},{7,8},{8,9},{9,10},{10,1... | collective-permute-start | bytes 196616 | tf_op jit(solution)/shard_map/ppermute | solution.py:556
  7.1 32.7 %copy-start.1 = (s32[2,512]{1,0:T(2,128)S(1)}, s32[2,512]{1,0:T(2,128)}, u32[]{:S(2)}) copy-start(s32[2,512]{1,0:T(2,128)} %param.15) | copy-start | bytes 12292
  7.1 32.7 %copy-start.3 = (f32[16]{0:T(128)S(1)}, f32[16]{0:T(128)}, u32[]{:S(2)}) copy-start(f32[16]{0:T(128)} %param.17) | copy-start | bytes 196
  7.1 32.8 %copy-start.4 = (s32[2]{0:T(128)S(1)}, s32[2]{0:T(128)}, u32[]{:S(2)}) copy-start(s32[2]{0:T(128)} %param.16) | copy-start | bytes 28
  7.1 41.4 %copy-start.2 = (s32[2,512]{1,0:T(2,128)S(1)}, s32[2,512]{1,0:T(2,128)}, u32[]{:S(2)}) copy-start(s32[2,512]{1,0:T(2,128)} %param.14) | copy-start | bytes 12292
  8.5 0.6 copy-start
  34.4 9.7 %collective-permute-start.1 = (f32[640,256]{1,0:T(8,128)S(1)}, f32[640,256]{1,0:T(8,128)S(1)}, u32[]{:S(2)}, u32[]{:S(2)}) collective-permute-start(f32[640,256]{1,0:T(8,128)S(1)} %all_gather.3), channel_id=1, source_target_pairs={{0,1},{1,2},{2,3},{3,4},{4,5},{5,6},{6,7},{7,8},{8,9},{9,10},{10,1... | collective-permute-start | bytes 1966088 | tf_op jit(solution)/shard_map/ppermute | solution.py:566
  36.0 36.0 %all-to-all-start = ((f32[16,2,2,32,128]{4,3,2,1,0:T(8,128)}), f32[16,2,2,32,128]{4,3,2,1,0:T(8,128)S(1)}, u32[]{:S(2)}, u32[]{:S(2)}) async-start(f32[16,2,2,32,128]{4,3,2,1,0:T(8,128)} %bitcast.15), calls=%async_computation | async-start | bytes 2097152 | tf_op jit(solution)/shard_map/all_to_all | solution.py:589
  44.2 6.5 %collective-permute-start.2 = (f32[640,256]{1,0:T(8,128)S(1)}, f32[640,256]{1,0:T(8,128)S(1)}, u32[]{:S(2)}, u32[]{:S(2)}) collective-permute-start(f32[640,256]{1,0:T(8,128)S(1)} %collective-permute-done.1), channel_id=1, source_target_pairs={{0,16},{16,0},{32,48},{48,32},{64,80},{80,64},{96,112},{112,96},{1... | collective-permute-start | bytes 1966088 | tf_op jit(solution)/shard_map/ppermute | solution.py:567

commit v2 on v1

--- a/solution.py
+++ b/solution.py
@@ -33,16 +33,13 @@
 
 
 def add_part(n, spot, block_ref, wsum_ref, bh, bl, old, old_rhs, new, new_rhs):
-    devices, rows, obs_tile = block_ref.shape
-    members = bl.shape[1]
-    mem_dev = members // devices
+    members, obs_tile = block_ref.shape
     top = 2 * PAD
-    block = block_ref[:, 0:mem_dev, :].reshape(members, obs_tile)
+    block = block_ref[...]
     mean = jnp.sum(block, axis=0, keepdims=True) * (1.0 / members)
-    value = block_ref[0, mem_dev : mem_dev + 1, :]
-    total = block_ref[0, mem_dev + 1 : mem_dev + 2, :] * wsum_ref[n : n + 1, spot]
+    total = wsum_ref[n : n + 1, spot]
     root = jnp.where(total > 0.0, jnp.sqrt(jnp.maximum(total, 1e-30)), 0.0)
-    row = jnp.broadcast_to(root * (value - mean), (PAD, obs_tile))
+    row = jnp.broadcast_to(-root * mean, (PAD, obs_tile))
     bh[n, 0:PAD, :], bh[n, PAD:top, :] = split(row)
     bh[n, top:, :], bl[n] = split((block - mean) * root)
     first = bh[n, 0 : top + HALF, :]
@@ -73,7 +70,7 @@
 
 
 def gram_part(which, block, wsum, members, sofar=()):
-    patches, obs_tile = wsum.shape[0], block.shape[2]
+    patches, obs_tile = wsum.shape[0], block.shape[1]
     spot = slice(which * obs_tile, (which + 1) * obs_tile)
     return pl.pallas_call(
         functools.partial(part_kernel, spot),
@@ -93,7 +90,7 @@
 def root_kernel(
     far_ref, wsum_ref, gram_ref, part_ref, out_ref, rhs_ref, bh, bl, t, p, ph, pl_, gh, gl, z, zh, zl
 ):
-    devices, _, obs_tile = far_ref.shape
+    obs_tile = far_ref.shape[1]
     patches, members = out_ref.shape[:2]
     inv = 1.0 / (members - 1)
     eye = (
@@ -323,7 +320,7 @@
 def inverse_roots(near, own, far, wsum, members):
     sofar = gram_part(1, own, wsum, members)
     sofar = gram_part(0, near, wsum, members, sofar)
-    patches, obs_tile = wsum.shape[0], far.shape[2]
+    patches, obs_tile = wsum.shape[0], far.shape[1]
     square = (patches, members, members)
     return pl.pallas_call(
         root_kernel,
@@ -486,8 +483,8 @@
             out_ref[line, lev] = done
             obs = jnp.where(source_row == lev * lines + line, pick(done), obs)
             old, old_next = now, now_next
-    message_ref[0:members, :] = obs
-    message_ref[members:, :] = partial_ref[members:, :]
+    value, rinv = partial_ref[members : members + 1, :], partial_ref[members + 1 : members + 2, :]
+    message_ref[...] = jnp.sqrt(rinv) * (obs - value)
 
 
 def edge_forecast(halo, edge, cells, partial, field):
@@ -499,15 +496,16 @@
 
     first = pl.BlockSpec((NSTEP, levels, mem_dev, nlat), lambda i: (0, 0, 0, 0))
     small = (halo, edge, cells, partial)
+    message = (mem_dev, partial.shape[1])
     return pl.pallas_call(
         functools.partial(edge_kernel, lines),
         grid=(1,),
         out_shape=(
             jax.ShapeDtypeStruct(field.shape, F32),
-            jax.ShapeDtypeStruct(partial.shape, F32),
+            jax.ShapeDtypeStruct(message, F32),
         ),
         in_specs=[whole(a) for a in small] + [pl.BlockSpec(memory_space=pl.ANY)],
-        out_specs=(first, whole(partial)),
+        out_specs=(first, pl.BlockSpec(message, lambda i: (0, 0))),
         input_output_aliases={len(small): 0},
         compiler_params=pltpu.CompilerParams(vmem_limit_bytes=60 * 1024 * 1024),
         cost_estimate=pl.CostEstimate(flops=10**7, bytes_accessed=10**6, transcendentals=0),
@@ -600,10 +598,7 @@
     places = jnp.arange(3 * obs_tile)
     wsum = jnp.sum(jnp.where(local_ids[:, :, None] == places, local_w[:, :, None], 0.0), 1)
 
-    shape = (devices, mem_dev + 8, obs_tile)
-    roots, rhs = inverse_roots(
-        near.reshape(shape), own.reshape(shape), far.reshape(shape), wsum, devices * mem_dev
-    )
+    roots, rhs = inverse_roots(near, own, far, wsum, devices * mem_dev)
     parts = apply_roots(roots, rhs, columns)
     return restore(lax.all_to_all(parts, "mem", 0, 0, tiled=True))
 

time: 108 us -> 106 us (0.981)
  waiting for transfers between devices: 5.51 us -> 4.06 us
  Pallas kernels: 31.6 us -> 30.2 us
  blocking collectives: 55.6 us -> 56.8 us
    all_to_all x1, blocking collectives: 32.1 us -> 33.6 us  [on_device(): return restore(lax.all_to_all(parts, 'mem', 0, 0, tiled=True))]
    ppermute x1, waiting for transfers between devices: 4.18 us -> 2.72 us  [neighbours(): near = lax.ppermute(value, ('mem', 'tile'), pairs)]
    pallas_call x1, Pallas kernels: 21.4 us -> 20.1 us  [inverse_roots(): pl.pallas_call(root_kernel, out_shape=(jax.ShapeDtypeStruct(square, F32),...]
  transfers between devices with their start and end apart: 4 -> 4, of which waited for: 2 -> 2; matrix products, arithmetic and copies ran while one was open for 1% -> 1% of each run, Pallas kernels for 25% -> 24%
where the time goes in v2:
time: 106 us; the launch traced here: 105 us
  blocking collectives  56.8 us (54%)
  Pallas kernels  30.2 us (28%)
  starting transfers between devices  11.9 us (11%)
  waiting for transfers between devices  4.06 us (4%)
  local copies, waits for them, and re-layouts  1.63 us (2%)
    all_to_all x1, blocking collectives, on_device(): return restore(lax.all_to_all(parts, 'mem', 0, 0, tiled=True))  33.6 us
    all_gather x1, blocking collectives, on_device(): own = lax.all_gather(message, 'mem', axis=0, tiled=True)  23.1 us
    pallas_call x1, Pallas kernels, inverse_roots(): pl.pallas_call(root_kernel, out_shape=(jax.ShapeDtypeStruct(square, F32),...  20.1 us
    ppermute x1, starting transfers between devices, neighbours(): far = lax.ppermute(near, 'mem', [(m, m ^ 1) for m in range(mem)])  4.34 us
    pallas_call x1, Pallas kernels, inner_forecast(): pl.pallas_call(inner_kernel, out_shape=(jax.ShapeDtypeStruct((lines, leve...  3.9 us
    all_to_all x1, starting transfers between devices, on_device(): lax.all_to_all(field.reshape(devices, lines // devices, levels, mem_dev,...  3.76 us
    ppermute x1, waiting for transfers between devices, neighbours(): near = lax.ppermute(value, ('mem', 'tile'), pairs)  2.72 us
    ppermute x1, starting transfers between devices, shifted(): return lax.ppermute(value, axis, pairs)  2.2 us
  transfers between devices with their start and end apart: 4, of which 2 were waited for; matrix products, arithmetic and copies ran while one was open for 1% of the time, Pallas kernels for 24%

profile of v2, /device:TPU:1, one launch (start us, length us, event | category | flops | bytes accessed | tf_op | source)
XLA Modules:
  0.0 105.5 jit_solution(17335730999595047351)
XLA Ops:
  0.0 1.0 slice.3
  1.0 2.2 %collective-permute-start = (f32[2,2,32,128]{3,2,1,0:T(8,128)S(1)}, f32[2,2,32,128]{3,2,1,0:T(8,128)S(1)}, u32[]{:S(2)}, u32[]{:S(2)}) collective-permute-start(f32[2,2,32,128]{3,2,1,0:T(8,128)S(1)} %bitcast.11), channel_id=1, source_target_pairs={{0,1},{1,2},{2,3},{3,4},{4,5},{5,6},{6,7},{7,8},{8,9},{9,10},{10,1... | collective-permute-start | bytes 196616 | tf_op jit(solution)/shard_map/ppermute | solution.py:554
  3.2 3.9 %shard_map.91 = (f32[32,2,32,128]{3,2,1,0:T(8,128)}, f32[3,2,32,128]{3,2,1,0:T(8,128)}, f32[40,256]{1,0:T(8,128)}, s32[8,256]{1,0:T(8,128)}) custom-call(f32[2048,128]{1,0:T(8,128)} %bitcast.10, f32[2,128]{1,0:T(2,128)} %courant_hbm.1, s32[1,256]{1,0:T(1,128)} %bitcast.12, f32[1,256]{1,0:T(1,128)} %bitcast.13, f32[1,256]{1,0:T(1,128)} %bitcast.14), custom_call_target="tpu_custom_call" | custom-call | flops 100000000 | bytes 2000000 | tf_op jit(solution)/shard_map/pallas_call | solution.py:446
  7.1 0.0 copy-start.1
  7.1 0.0 copy-start.3
  7.1 0.0 copy-start.2
  7.1 0.0 copy-start.4
  7.2 1.3 %collective-permute-done.halo_ref = f32[2,2,32,128]{3,2,1,0:T(8,128)S(1)} collective-permute-done((f32[2,2,32,128]{3,2,1,0:T(8,128)S(1)}, f32[2,2,32,128]{3,2,1,0:T(8,128)S(1)}, u32[]{:S(2)}, u32[]{:S(2)}) %collective-permute-start) | collective-permute-done | bytes 65568 | tf_op jit(solution)/shard_map/ppermute | solution.py:554
  8.5 0.0 copy-start
  8.5 0.6 copy-done
  9.1 1.8 %shard_map.92 = (f32[32,2,32,128]{3,2,1,0:T(8,128)}, f32[32,256]{1,0:T(8,128)}) custom-call(f32[2,2,32,128]{3,2,1,0:T(8,128)} %copy-done, f32[3,2,32,128]{3,2,1,0:T(8,128)} %get-tuple-element.23.edge_ref, s32[8,256]{1,0:T(8,128)} %get-tuple-element.24.cell_ref, f32[40,256]{1,0:T(8,128)} %get-tuple-element.25.partial_ref, ...), custom_call_target="tpu_custom_call", output_to_operand_aliasing={{0}: (4, {})} | custom-call | flops 10000000 | bytes 1000000 | tf_op jit(solution)/shard_map/pallas_call | solution.py:500
  10.9 23.1 %all_gather.3.block_ref = f32[512,256]{1,0:T(8,128)S(1)} all-gather(f32[32,256]{1,0:T(8,128)} %get-tuple-element.27), channel_id=1, replica_groups=mesh['mem'=16,'tile'=16] {'mem'}, dimensions={0}, use_global_device_ids=true | all-gather | bytes 557056 | tf_op jit(solution)/shard_map/all_gather | solution.py:582
  34.1 1.6 %collective-permute-start.1 = (f32[512,256]{1,0:T(8,128)S(1)}, f32[512,256]{1,0:T(8,128)S(1)}, u32[]{:S(2)}, u32[]{:S(2)}) collective-permute-start(f32[512,256]{1,0:T(8,128)S(1)} %all_gather.3.block_ref), channel_id=1, source_target_pairs={{0,1},{1,2},{2,3},{3,4},{4,5},{5,6},{6,7},{7,8},{8,9},{9,10},{10,1... | collective-permute-start | bytes 1572872 | tf_op jit(solution)/shard_map/ppermute | solution.py:564
  35.7 3.8 %all-to-all-start = ((f32[16,2,2,32,128]{4,3,2,1,0:T(8,128)}), f32[16,2,2,32,128]{4,3,2,1,0:T(8,128)S(1)}, u32[]{:S(2)}, u32[]{:S(2)}) async-start(f32[16,2,2,32,128]{4,3,2,1,0:T(8,128)} %bitcast.9), calls=%async_computation | async-start | bytes 2097152 | tf_op jit(solution)/shard_map/all_to_all | solution.py:587
  39.4 0.0 copy-done.1
  39.4 0.0 copy-done.3
  39.5 0.1 select_reduce_fusion.1
  39.5 0.0 copy-done.2
  39.6 0.0 copy-done.4
  39.6 0.1 compare_select_fusion.2
  39.7 2.7 %collective-permute-done.1.block_ref = f32[512,256]{1,0:T(8,128)S(1)} collective-permute-done((f32[512,256]{1,0:T(8,128)S(1)}, f32[512,256]{1,0:T(8,128)S(1)}, u32[]{:S(2)}, u32[]{:S(2)}) %collective-permute-start.1) | collective-permute-done | bytes 524320 | tf_op jit(solution)/shard_map/ppermute | solution.py:564
  42.4 4.3 %collective-permute-start.2 = (f32[512,256]{1,0:T(8,128)S(1)}, f32[512,256]{1,0:T(8,128)S(1)}, u32[]{:S(2)}, u32[]{:S(2)}) collective-permute-start(f32[512,256]{1,0:T(8,128)S(1)} %collective-permute-done.1.block_ref), channel_id=1, source_target_pairs={{0,16},{16,0},{32,48},{48,32},{64,80},{80,64},{96,112},{112,96},{1... | collective-permute-start | bytes 1572872 | tf_op jit(solution)/shard_map/ppermute | solution.py:565
  46.7 0.4 select_reduce_fusion.wsum_ref
  47.1 0.8 shard_map.93
  48.0 0.8 shard_map.94
  48.8 0.0 collective-permute-done.2.far_ref
  48.8 20.1 %shard_map.95 = (f32[2,512,512]{2,1,0:T(8,128)S(1)}, f32[2,8,512]{2,1,0:T(8,128)S(1)}) custom-call(f32[512,256]{1,0:T(8,128)S(1)} %collective-permute-done.2.far_ref, f32[2,768]{1,0:T(2,128)S(1)} %select_reduce_fusion.wsum_ref, f32[2,512,512]{2,1,0:T(8,128)S(1)} %get-tuple-element.36.gram_ref, f32[2,8,512]{2,1,0:T(8,128)S(1)} %get-tuple-element.37.part_ref), custom_call_target="tpu_custom_call" | custom-call | flops 24999999488 | bytes 4000000 | tf_op jit(solution)/shard_map/pallas_call | solution.py:325
  68.9 0.0 all-to-all-done.cols_ref
  68.9 1.2 %shard_map.96 = f32[16,2,2,32,128]{4,3,2,1,0:T(8,128)S(1)} custom-call(f32[2,512,512]{2,1,0:T(8,128)S(1)} %get-tuple-element.38.root_ref, f32[2,8,512]{2,1,0:T(8,128)S(1)} %get-tuple-element.39.rhs_ref, f32[16,2,2,32,128]{4,3,2,1,0:T(8,128)S(1)} %all-to-all-done.cols_ref), custom_call_target="tpu_custom_call" | custom-call | flops 800000000 | bytes 4000000 | tf_op jit(solution)/shard_map/pallas_call | solution.py:369
  70.1 33.6 %all_to_all.10.part_ref = f32[16,2,2,32,128]{4,3,2,1,0:T(8,128)S(1)} all-to-all(f32[16,2,2,32,128]{4,3,2,1,0:T(8,128)S(1)} %shard_map.96), channel_id=1, replica_groups=mesh['mem'=16,'tile'=16] {'mem'}, dimensions={0} | all-to-all | bytes 2097152 | tf_op jit(solution)/shard_map/all_to_all | solution.py:603
  103.7 1.6 %shard_map.97 = f32[2048,128]{1,0:T(8,128)} custom-call(f32[16,2,2,32,128]{4,3,2,1,0:T(8,128)S(1)} %all_to_all.10.part_ref), custom_call_target="tpu_custom_call" | custom-call | tf_op jit(solution)/shard_map/pallas_call | solution.py:537
  (2 shorter events, 0.0 us)
Async XLA Ops:
  1.0 7.5 %collective-permute-start = (f32[2,2,32,128]{3,2,1,0:T(8,128)S(1)}, f32[2,2,32,128]{3,2,1,0:T(8,128)S(1)}, u32[]{:S(2)}, u32[]{:S(2)}) collective-permute-start(f32[2,2,32,128]{3,2,1,0:T(8,128)S(1)} %bitcast.11), channel_id=1, source_target_pairs={{0,1},{1,2},{2,3},{3,4},{4,5},{5,6},{6,7},{7,8},{8,9},{9,10},{10,1... | collective-permute-start | bytes 196616 | tf_op jit(solution)/shard_map/ppermute | solution.py:554
  7.1 32.3 %copy-start.1 = (s32[2,512]{1,0:T(2,128)S(1)}, s32[2,512]{1,0:T(2,128)}, u32[]{:S(2)}) copy-start(s32[2,512]{1,0:T(2,128)} %param.15) | copy-start | bytes 12292
  7.1 32.3 %copy-start.3 = (f32[16]{0:T(128)S(1)}, f32[16]{0:T(128)}, u32[]{:S(2)}) copy-start(f32[16]{0:T(128)} %param.17) | copy-start | bytes 196
  7.1 32.4 %copy-start.2 = (s32[2,512]{1,0:T(2,128)S(1)}, s32[2,512]{1,0:T(2,128)}, u32[]{:S(2)}) copy-start(s32[2,512]{1,0:T(2,128)} %param.14) | copy-start | bytes 12292
  7.1 32.4 %copy-start.4 = (s32[2]{0:T(128)S(1)}, s32[2]{0:T(128)}, u32[]{:S(2)}) copy-start(s32[2]{0:T(128)} %param.16) | copy-start | bytes 28
  8.5 0.6 copy-start
  34.1 8.3 %collective-permute-start.1 = (f32[512,256]{1,0:T(8,128)S(1)}, f32[512,256]{1,0:T(8,128)S(1)}, u32[]{:S(2)}, u32[]{:S(2)}) collective-permute-start(f32[512,256]{1,0:T(8,128)S(1)} %all_gather.3.block_ref), channel_id=1, source_target_pairs={{0,1},{1,2},{2,3},{3,4},{4,5},{5,6},{6,7},{7,8},{8,9},{9,10},{10,1... | collective-permute-start | bytes 1572872 | tf_op jit(solution)/shard_map/ppermute | solution.py:564
  35.7 33.2 %all-to-all-start = ((f32[16,2,2,32,128]{4,3,2,1,0:T(8,128)}), f32[16,2,2,32,128]{4,3,2,1,0:T(8,128)S(1)}, u32[]{:S(2)}, u32[]{:S(2)}) async-start(f32[16,2,2,32,128]{4,3,2,1,0:T(8,128)} %bitcast.9), calls=%async_computation | async-start | bytes 2097152 | tf_op jit(solution)/shard_map/all_to_all | solution.py:587
  42.4 6.4 %collective-permute-start.2 = (f32[512,256]{1,0:T(8,128)S(1)}, f32[512,256]{1,0:T(8,128)S(1)}, u32[]{:S(2)}, u32[]{:S(2)}) collective-permute-start(f32[512,256]{1,0:T(8,128)S(1)} %collective-permute-done.1.block_ref), channel_id=1, source_target_pairs={{0,16},{16,0},{32,48},{48,32},{64,80},{80,64},{96,112},{112,96},{1... | collective-permute-start | bytes 1572872 | tf_op jit(solution)/shard_map/ppermute | solution.py:565

commit v3 on v2

--- a/solution.py
+++ b/solution.py
@@ -388,33 +388,14 @@
     return lambda value: mm(jnp.concatenate(split(value), 1), twice)
 
 
-def inner_kernel(
-    field_hbm, courant_hbm, cell_hbm, value_hbm, rinv_hbm, out_ref, edge_ref, message_ref, extra_ref,
-    field_ref, courant_ref, cell_ref, value_ref, rinv_ref, sems
-):
-    copies = [
-        pltpu.make_async_copy(source, target, sems.at[i])
-        for i, (source, target) in enumerate(
-            (
-                (field_hbm, field_ref),
-                (courant_hbm, courant_ref),
-                (cell_hbm, cell_ref),
-                (value_hbm, value_ref),
-                (rinv_hbm, rinv_ref),
-            )
-        )
-    ]
-    for copy in copies:
-        copy.start()
-    for copy in copies:
-        copy.wait()
+def inner_kernel(field_ref, pack_ref, out_ref, edge_ref, obs_ref):
     lines, levels, members, nlat = out_ref.shape
-    cells = cell_ref[...]
+    cells = pack_ref[2:3, :].astype(jnp.int32)
     pick = picker(cells, nlat)
     source_row = cells // nlat
-    obs = jnp.zeros((members, cells.shape[1]), F32)
+    obs = jnp.zeros(obs_ref.shape, F32)
     for lev in range(levels):
-        courant = courant_ref[lev : lev + 1, :]
+        courant = pack_ref[3:4, lev * nlat : (lev + 1) * nlat]
         old, old_next = None, None
         for line in range(lines):
             now = field_ref[pl.ds(lev * lines + line, members, stride=levels * lines), :]
@@ -428,52 +409,33 @@
                 out_ref[line, lev] = done
                 obs = jnp.where(source_row == lev * lines + line, pick(done), obs)
             old, old_next = now, now_next
-    message_ref[0:members, :] = obs
-    message_ref[members : members + 1, :] = value_ref[...]
-    message_ref[members + 1 : members + 2, :] = rinv_ref[...]
-    message_ref[members + 2 :, :] = jnp.zeros((6, obs.shape[1]), F32)
-    extra_ref[...] = jnp.zeros(extra_ref.shape, jnp.int32)
-    extra_ref[0:1, :] = cells
-    edge_ref[NSTEP] = jnp.zeros(edge_ref.shape[1:], F32)
-    for lev in range(levels):
-        edge_ref[NSTEP, lev, 0:1, :] = courant_ref[lev : lev + 1, :]
-
-
-def inner_forecast(members, courant, cells, value, rinv):
+    obs_ref[...] = obs
+
+
+def inner_forecast(members, pack):
     mem_dev, levels, lines, nlat = members.shape
     rows = mem_dev * levels * lines
-    nobs = cells.shape[1]
     return pl.pallas_call(
         inner_kernel,
         out_shape=(
             jax.ShapeDtypeStruct((lines, levels, mem_dev, nlat), F32),
-            jax.ShapeDtypeStruct((NSTEP + 1, levels, mem_dev, nlat), F32),
-            jax.ShapeDtypeStruct((mem_dev + 8, nobs), F32),
-            jax.ShapeDtypeStruct((8, nobs), jnp.int32),
+            jax.ShapeDtypeStruct((NSTEP, levels, mem_dev, nlat), F32),
+            jax.ShapeDtypeStruct((mem_dev, pack.shape[1]), F32),
         ),
-        in_specs=[pl.BlockSpec(memory_space=pltpu.HBM)] * 5,
-        scratch_shapes=[
-            pltpu.VMEM((rows, nlat), F32),
-            pltpu.VMEM(courant.shape, F32),
-            pltpu.VMEM(cells.shape, jnp.int32),
-            pltpu.VMEM(value.shape, F32),
-            pltpu.VMEM(rinv.shape, F32),
-            pltpu.SemaphoreType.DMA((5,)),
-        ],
-        compiler_params=pltpu.CompilerParams(vmem_limit_bytes=60 * 1024 * 1024),
+        compiler_params=pltpu.CompilerParams(vmem_limit_bytes=24 * 1024 * 1024),
         cost_estimate=pl.CostEstimate(flops=10**8, bytes_accessed=2 * 10**6, transcendentals=0),
-    )(members.reshape(rows, nlat), courant, cells, value, rinv)
-
-
-def edge_kernel(lines, halo_ref, edge_ref, cell_ref, partial_ref, field_ref, out_ref, message_ref):
+    )(members.reshape(rows, nlat), pack)
+
+
+def edge_kernel(lines, halo_ref, edge_ref, pack_ref, partial_ref, field_ref, out_ref, message_ref):
     del field_ref
     _, levels, members, nlat = edge_ref.shape
-    cells = cell_ref[0:1, :]
+    cells = pack_ref[2:3, :].astype(jnp.int32)
     pick = picker(cells, nlat)
     source_row = cells // nlat
-    obs = partial_ref[0:members, :]
+    obs = partial_ref[...]
     for lev in range(levels):
-        courant = edge_ref[NSTEP, lev, 0:1, :]
+        courant = pack_ref[3:4, lev * nlat : (lev + 1) * nlat]
         old = halo_ref[1, lev]
         old_next = advance(old, halo_ref[0, lev], courant)
         for line in range(NSTEP):
@@ -483,11 +445,10 @@
             out_ref[line, lev] = done
             obs = jnp.where(source_row == lev * lines + line, pick(done), obs)
             old, old_next = now, now_next
-    value, rinv = partial_ref[members : members + 1, :], partial_ref[members + 1 : members + 2, :]
-    message_ref[...] = jnp.sqrt(rinv) * (obs - value)
-
-
-def edge_forecast(halo, edge, cells, partial, field):
+    message_ref[...] = jnp.sqrt(pack_ref[1:2, :]) * (obs - pack_ref[0:1, :])
+
+
+def edge_forecast(halo, edge, pack, partial, field):
     lines, levels, mem_dev, nlat = field.shape
 
     def whole(array):
@@ -495,19 +456,18 @@
         return pl.BlockSpec(array.shape, lambda i: zeros)
 
     first = pl.BlockSpec((NSTEP, levels, mem_dev, nlat), lambda i: (0, 0, 0, 0))
-    small = (halo, edge, cells, partial)
-    message = (mem_dev, partial.shape[1])
+    small = (halo, edge, pack, partial)
     return pl.pallas_call(
         functools.partial(edge_kernel, lines),
         grid=(1,),
         out_shape=(
             jax.ShapeDtypeStruct(field.shape, F32),
-            jax.ShapeDtypeStruct(message, F32),
+            jax.ShapeDtypeStruct(partial.shape, F32),
         ),
         in_specs=[whole(a) for a in small] + [pl.BlockSpec(memory_space=pl.ANY)],
-        out_specs=(first, pl.BlockSpec(message, lambda i: (0, 0))),
+        out_specs=(first, whole(partial)),
         input_output_aliases={len(small): 0},
-        compiler_params=pltpu.CompilerParams(vmem_limit_bytes=60 * 1024 * 1024),
+        compiler_params=pltpu.CompilerParams(vmem_limit_bytes=24 * 1024 * 1024),
         cost_estimate=pl.CostEstimate(flops=10**7, bytes_accessed=10**6, transcendentals=0),
     )(*small, field)
 
@@ -575,10 +535,10 @@
     slots = nbr_obs.shape[1]
     edge = jnp.transpose(members[:, :, lines - NSTEP :, :], (2, 1, 0, 3))
     halo = shifted(edge, "tile", 1)
-    field, first_lines, partial, cells = inner_forecast(
-        members, courant, obs_cell[None], obs_value[None], obs_rinv[None]
-    )
-    field, message = edge_forecast(halo, first_lines, cells, partial, field)
+    rows = [obs_value, obs_rinv, obs_cell.astype(F32), courant.reshape(-1)]
+    pack = jnp.concatenate([row[None] for row in rows] + [jnp.zeros((4, obs_tile), F32)], 0)
+    field, first_lines, partial = inner_forecast(members, pack)
+    field, message = edge_forecast(halo, first_lines, pack, partial, field)
     own = lax.all_gather(message, "mem", axis=0, tiled=True)
     own, nbr_obs, nbr_class, nbr_count, loc_table, field = lax.optimization_barrier(
         (own, nbr_obs, nbr_class, nbr_count, loc_table, field)

time: 106 us -> 104 us (0.981)
  waiting for transfers between devices: 4.06 us -> 2.16 us
  local copies, waits for them, and re-layouts: 1.63 us -> 2.95 us
  blocking collectives: 56.8 us -> 55.6 us
    pallas_call x1, Pallas kernels: 20.1 us -> 21.4 us  [inverse_roots(): pl.pallas_call(root_kernel, out_shape=(jax.ShapeDtypeStruct(square, F32),...]
    ppermute x1, waiting for transfers between devices: 1.33 us -> 0.02 us  [shifted(): return lax.ppermute(value, axis, pairs)]
    pallas_call x1, Pallas kernels: 3.9 us -> 2.61 us  [inner_forecast(): pl.pallas_call(inner_kernel, out_shape=(jax.ShapeDtypeStruct((lines, leve...]
    ppermute x1, starting transfers between devices: 1.61 us -> 2.76 us  [neighbours(): near = lax.ppermute(value, ('mem', 'tile'), pairs)]
  transfers between devices with their start and end apart: 4 -> 4, of which waited for: 2 -> 1; matrix products, arithmetic and copies ran while one was open for 1% -> 2% of each run, Pallas kernels for 24% -> 25%
where the time goes in v3:
time: 104 us
  blocking collectives  55.6 us (53%)
  Pallas kernels  29.3 us (28%)
  starting transfers between devices  12.5 us (12%)
  local copies, waits for them, and re-layouts  2.95 us (3%)
  waiting for transfers between devices  2.16 us (2%)
  other arithmetic  1.27 us (1%)
    all_to_all x1, blocking collectives, on_device(): return restore(lax.all_to_all(parts, 'mem', 0, 0, tiled=True))  32.7 us
    all_gather x1, blocking collectives, on_device(): own = lax.all_gather(message, 'mem', axis=0, tiled=True)  22.9 us
    pallas_call x1, Pallas kernels, inverse_roots(): pl.pallas_call(root_kernel, out_shape=(jax.ShapeDtypeStruct(square, F32),...  21.4 us
    ppermute x1, starting transfers between devices, neighbours(): far = lax.ppermute(near, 'mem', [(m, m ^ 1) for m in range(mem)])  3.78 us
    all_to_all x1, starting transfers between devices, on_device(): lax.all_to_all(field.reshape(devices, lines // devices, levels, mem_dev,...  3.76 us
    ppermute x1, starting transfers between devices, neighbours(): near = lax.ppermute(value, ('mem', 'tile'), pairs)  2.76 us
    pallas_call x1, Pallas kernels, inner_forecast(): pl.pallas_call(inner_kernel, out_shape=(jax.ShapeDtypeStruct((lines, leve...  2.61 us
    ppermute x1, starting transfers between devices, shifted(): return lax.ppermute(value, axis, pairs)  2.2 us
  transfers between devices with their start and end apart: 4, of which 1 were waited for; matrix products, arithmetic and copies ran while one was open for 2% of the time, Pallas kernels for 25%

profile of v3, /device:TPU:1, one launch (start us, length us, event | category | flops | bytes accessed | tf_op | source)
XLA Modules:
  0.0 104.1 jit_solution(14713659758547643384)
XLA Ops:
  0.0 1.0 slice.3
  1.0 2.2 %collective-permute-start = (f32[2,2,32,128]{3,2,1,0:T(8,128)S(1)}, f32[2,2,32,128]{3,2,1,0:T(8,128)S(1)}, u32[]{:S(2)}, u32[]{:S(2)}) collective-permute-start(f32[2,2,32,128]{3,2,1,0:T(8,128)S(1)} %bitcast.11), channel_id=1, source_target_pairs={{0,1},{1,2},{2,3},{3,4},{4,5},{5,6},{6,7},{7,8},{8,9},{9,10},{10,1... | collective-permute-start | bytes 196616 | tf_op jit(solution)/shard_map/ppermute | solution.py:514
  3.2 0.7 convert_element_type.3
  3.9 0.7 concatenate.3.pack_ref
  4.6 0.0 copy-start
  4.6 1.2 %copy-done = f32[32,2,32,128]{3,2,1,0:T(8,128)S(1)} copy-done((f32[32,2,32,128]{3,2,1,0:T(8,128)S(1)}, f32[32,2,32,128]{3,2,1,0:T(8,128)}, u32[]{:S(2)}) %copy-start) | copy-done | bytes 1048600
  5.8 2.6 %shard_map.91 = (f32[32,2,32,128]{3,2,1,0:T(8,128)}, f32[2,2,32,128]{3,2,1,0:T(8,128)S(1)}, f32[32,256]{1,0:T(8,128)S(1)}) custom-call(f32[2048,128]{1,0:T(8,128)S(1)} %bitcast.10, f32[8,256]{1,0:T(8,128)S(1)} %concatenate.3.pack_ref), custom_call_target="tpu_custom_call" | custom-call | flops 100000000 | bytes 2000000 | tf_op jit(solution)/shard_map/pallas_call | solution.py:418
  8.5 0.0 copy-start.3
  8.5 0.0 copy-start.2
  8.5 0.0 copy-start.4
  8.5 0.0 collective-permute-done.halo_ref
  8.5 0.8 shard_map.92
  9.3 22.9 %all_gather.3.block_ref = f32[512,256]{1,0:T(8,128)S(1)} all-gather(f32[32,256]{1,0:T(8,128)S(1)} %get-tuple-element.25), channel_id=1, replica_groups=mesh['mem'=16,'tile'=16] {'mem'}, dimensions={0}, use_global_device_ids=true | all-gather | bytes 557056 | tf_op jit(solution)/shard_map/all_gather | solution.py:542
  32.2 2.8 %collective-permute-start.1 = (f32[512,256]{1,0:T(8,128)S(1)}, f32[512,256]{1,0:T(8,128)S(1)}, u32[]{:S(2)}, u32[]{:S(2)}) collective-permute-start(f32[512,256]{1,0:T(8,128)S(1)} %all_gather.3.block_ref), channel_id=1, source_target_pairs={{0,1},{1,2},{2,3},{3,4},{4,5},{5,6},{6,7},{7,8},{8,9},{9,10},{10,1... | collective-permute-start | bytes 1572872 | tf_op jit(solution)/shard_map/ppermute | solution.py:524
  35.0 3.8 %all-to-all-start = ((f32[16,2,2,32,128]{4,3,2,1,0:T(8,128)}), f32[16,2,2,32,128]{4,3,2,1,0:T(8,128)S(1)}, u32[]{:S(2)}, u32[]{:S(2)}) async-start(f32[16,2,2,32,128]{4,3,2,1,0:T(8,128)} %bitcast.6), calls=%async_computation | async-start | bytes 2097152 | tf_op jit(solution)/shard_map/all_to_all | solution.py:547
  38.7 0.0 copy-done.1
  38.7 0.0 copy-done.3
  38.7 0.1 select_reduce_fusion.1
  38.8 0.0 copy-done.2
  38.9 0.0 copy-done.4
  38.9 0.1 compare_select_fusion.2
  39.0 2.1 %collective-permute-done.1.block_ref = f32[512,256]{1,0:T(8,128)S(1)} collective-permute-done((f32[512,256]{1,0:T(8,128)S(1)}, f32[512,256]{1,0:T(8,128)S(1)}, u32[]{:S(2)}, u32[]{:S(2)}) %collective-permute-start.1) | collective-permute-done | bytes 524320 | tf_op jit(solution)/shard_map/ppermute | solution.py:524
  41.1 3.8 %collective-permute-start.2 = (f32[512,256]{1,0:T(8,128)S(1)}, f32[512,256]{1,0:T(8,128)S(1)}, u32[]{:S(2)}, u32[]{:S(2)}) collective-permute-start(f32[512,256]{1,0:T(8,128)S(1)} %collective-permute-done.1.block_ref), channel_id=1, source_target_pairs={{0,16},{16,0},{32,48},{48,32},{64,80},{80,64},{96,112},{112,96},{1... | collective-permute-start | bytes 1572872 | tf_op jit(solution)/shard_map/ppermute | solution.py:525
  44.9 0.4 select_reduce_fusion.wsum_ref
  45.3 0.8 shard_map.93
  46.1 0.9 shard_map.94
  47.0 0.0 collective-permute-done.2.far_ref
  47.0 21.4 %shard_map.95 = (f32[2,512,512]{2,1,0:T(8,128)S(1)}, f32[2,8,512]{2,1,0:T(8,128)S(1)}) custom-call(f32[512,256]{1,0:T(8,128)S(1)} %collective-permute-done.2.far_ref, f32[2,768]{1,0:T(2,128)S(1)} %select_reduce_fusion.wsum_ref, f32[2,512,512]{2,1,0:T(8,128)S(1)} %get-tuple-element.34.gram_ref, f32[2,8,512]{2,1,0:T(8,128)S(1)} %get-tuple-element.35.part_ref), custom_call_target="tpu_custom_call" | custom-call | flops 24999999488 | bytes 4000000 | tf_op jit(solution)/shard_map/pallas_call | solution.py:325
  68.4 0.0 all-to-all-done.cols_ref
  68.4 1.2 %shard_map.96 = f32[16,2,2,32,128]{4,3,2,1,0:T(8,128)S(1)} custom-call(f32[2,512,512]{2,1,0:T(8,128)S(1)} %get-tuple-element.36.root_ref, f32[2,8,512]{2,1,0:T(8,128)S(1)} %get-tuple-element.37.rhs_ref, f32[16,2,2,32,128]{4,3,2,1,0:T(8,128)S(1)} %all-to-all-done.cols_ref), custom_call_target="tpu_custom_call" | custom-call | flops 800000000 | bytes 4000000 | tf_op jit(solution)/shard_map/pallas_call | solution.py:369
  69.6 32.7 %all_to_all.10.part_ref = f32[16,2,2,32,128]{4,3,2,1,0:T(8,128)S(1)} all-to-all(f32[16,2,2,32,128]{4,3,2,1,0:T(8,128)S(1)} %shard_map.96), channel_id=1, replica_groups=mesh['mem'=16,'tile'=16] {'mem'}, dimensions={0} | all-to-all | bytes 2097152 | tf_op jit(solution)/shard_map/all_to_all | solution.py:563
  102.3 1.6 %shard_map.97 = f32[2048,128]{1,0:T(8,128)} custom-call(f32[16,2,2,32,128]{4,3,2,1,0:T(8,128)S(1)} %all_to_all.10.part_ref), custom_call_target="tpu_custom_call" | custom-call | tf_op jit(solution)/shard_map/pallas_call | solution.py:497
  (4 shorter events, 0.0 us)
Async XLA Ops:
  1.0 7.5 %collective-permute-start = (f32[2,2,32,128]{3,2,1,0:T(8,128)S(1)}, f32[2,2,32,128]{3,2,1,0:T(8,128)S(1)}, u32[]{:S(2)}, u32[]{:S(2)}) collective-permute-start(f32[2,2,32,128]{3,2,1,0:T(8,128)S(1)} %bitcast.11), channel_id=1, source_target_pairs={{0,1},{1,2},{2,3},{3,4},{4,5},{5,6},{6,7},{7,8},{8,9},{9,10},{10,1... | collective-permute-start | bytes 196616 | tf_op jit(solution)/shard_map/ppermute | solution.py:514
  4.6 1.2 %copy-start = (f32[32,2,32,128]{3,2,1,0:T(8,128)S(1)}, f32[32,2,32,128]{3,2,1,0:T(8,128)}, u32[]{:S(2)}) copy-start(f32[32,2,32,128]{3,2,1,0:T(8,128)} %param.9) | copy-start | bytes 3145732
  8.5 30.3 %copy-start.1 = (s32[2,512]{1,0:T(2,128)S(1)}, s32[2,512]{1,0:T(2,128)}, u32[]{:S(2)}) copy-start(s32[2,512]{1,0:T(2,128)} %param.15) | copy-start | bytes 12292
  8.5 30.3 %copy-start.3 = (f32[16]{0:T(128)S(1)}, f32[16]{0:T(128)}, u32[]{:S(2)}) copy-start(f32[16]{0:T(128)} %param.17) | copy-start | bytes 196
  8.5 30.4 %copy-start.2 = (s32[2,512]{1,0:T(2,128)S(1)}, s32[2,512]{1,0:T(2,128)}, u32[]{:S(2)}) copy-start(s32[2,512]{1,0:T(2,128)} %param.14) | copy-start | bytes 12292
  8.5 30.4 %copy-start.4 = (s32[2]{0:T(128)S(1)}, s32[2]{0:T(128)}, u32[]{:S(2)}) copy-start(s32[2]{0:T(128)} %param.16) | copy-start | bytes 28
  32.2 8.9 %collective-permute-start.1 = (f32[512,256]{1,0:T(8,128)S(1)}, f32[512,256]{1,0:T(8,128)S(1)}, u32[]{:S(2)}, u32[]{:S(2)}) collective-permute-start(f32[512,256]{1,0:T(8,128)S(1)} %all_gather.3.block_ref), channel_id=1, source_target_pairs={{0,1},{1,2},{2,3},{3,4},{4,5},{5,6},{6,7},{7,8},{8,9},{9,10},{10,1... | collective-permute-start | bytes 1572872 | tf_op jit(solution)/shard_map/ppermute | solution.py:524
  35.0 33.4 %all-to-all-start = ((f32[16,2,2,32,128]{4,3,2,1,0:T(8,128)}), f32[16,2,2,32,128]{4,3,2,1,0:T(8,128)S(1)}, u32[]{:S(2)}, u32[]{:S(2)}) async-start(f32[16,2,2,32,128]{4,3,2,1,0:T(8,128)} %bitcast.6), calls=%async_computation | async-start | bytes 2097152 | tf_op jit(solution)/shard_map/all_to_all | solution.py:547
  41.1 5.9 %collective-permute-start.2 = (f32[512,256]{1,0:T(8,128)S(1)}, f32[512,256]{1,0:T(8,128)S(1)}, u32[]{:S(2)}, u32[]{:S(2)}) collective-permute-start(f32[512,256]{1,0:T(8,128)S(1)} %collective-permute-done.1.block_ref), channel_id=1, source_target_pairs={{0,16},{16,0},{32,48},{48,32},{64,80},{80,64},{96,112},{112,96},{1... | collective-permute-start | bytes 1572872 | tf_op jit(solution)/shard_map/ppermute | solution.py:525

commit v4 on v3

--- a/solution.py
+++ b/solution.py
@@ -88,10 +88,10 @@
 
 
 def root_kernel(
-    far_ref, wsum_ref, gram_ref, part_ref, out_ref, rhs_ref, bh, bl, t, p, ph, pl_, gh, gl, z, zh, zl
+    far_ref, wsum_ref, gram_ref, part_ref, high_ref, low_ref, weight_ref, rhs_ref, bh, bl, t, p, ph, pl_, gh, gl, z, zh, zl
 ):
     obs_tile = far_ref.shape[1]
-    patches, members = out_ref.shape[:2]
+    patches, members = high_ref.shape[:2]
     inv = 1.0 / (members - 1)
     eye = (
         lax.broadcasted_iota(jnp.int32, (HALF, HALF), 0)
@@ -300,11 +300,14 @@
 
     def finish(make):
         for n in every:
-            z00, z10, z11 = make(n)
-            out_ref[n, LO, LO] = z00 * lax.rsqrt(scales[n])
-            out_ref[n, HI, LO] = z10 * lax.rsqrt(scales[n])
-            out_ref[n, LO, HI] = z10.T * lax.rsqrt(scales[n])
-            out_ref[n, HI, HI] = z11 * lax.rsqrt(scales[n])
+            small = lax.rsqrt(scales[n])
+            z00, z10, z11 = (part * small for part in make(n))
+            first, last = rhs_ref[n, 0:1, LO], rhs_ref[n, 0:1, HI]
+            for rows, parts in ((LO, (z00, z10.T)), (HI, (z10, z11))):
+                for cols, part in zip((LO, HI), parts):
+                    put(part, None, high_ref, low_ref, n, rows, cols)
+                total = parts[0] * first + parts[1] * last
+                weight_ref[n, rows, :] = jnp.sum(total, axis=1, keepdims=True)
 
     @pl.when(1.0 - least > LOW)
     def _():
@@ -325,7 +328,9 @@
     return pl.pallas_call(
         root_kernel,
         out_shape=(
-            jax.ShapeDtypeStruct(square, F32),
+            jax.ShapeDtypeStruct(square, BF),
+            jax.ShapeDtypeStruct(square, BF),
+            jax.ShapeDtypeStruct((patches, members, 1), F32),
             jax.ShapeDtypeStruct((patches, 8, members), F32),
         ),
         scratch_shapes=[
@@ -346,13 +351,11 @@
     )(far, wsum, *sofar)
 
 
-def apply_kernel(root_ref, rhs_ref, cols_ref, out_ref):
+def apply_kernel(high_ref, low_ref, weight_ref, cols_ref, out_ref):
     devices, patches, levels, mem_dev, nlat = cols_ref.shape
     members = devices * mem_dev
     for n in range(patches):
-        root = root_ref[n]
-        high, low = split(root)
-        weight = jnp.sum(root * rhs_ref[n, 0:1, :], axis=1, keepdims=True)
+        high, low, weight = high_ref[n], low_ref[n], weight_ref[n]
         cols = jnp.concatenate(
             [cols_ref[:, n, lev].reshape(members, nlat) for lev in range(levels)], 1
         )
@@ -365,13 +368,13 @@
             out_ref[:, n, lev] = part.reshape(devices, mem_dev, nlat)
 
 
-def apply_roots(roots, rhs, cols):
+def apply_roots(high, low, weight, cols):
     return pl.pallas_call(
         apply_kernel,
         out_shape=jax.ShapeDtypeStruct(cols.shape, F32),
         compiler_params=pltpu.CompilerParams(vmem_limit_bytes=24 * 1024 * 1024),
         cost_estimate=pl.CostEstimate(flops=8 * 10**8, bytes_accessed=4 * 10**6, transcendentals=0),
-    )(roots, rhs, cols)
+    )(high, low, weight, cols)
 
 
 def advance(field, west, courant):
@@ -558,8 +561,8 @@
     places = jnp.arange(3 * obs_tile)
     wsum = jnp.sum(jnp.where(local_ids[:, :, None] == places, local_w[:, :, None], 0.0), 1)
 
-    roots, rhs = inverse_roots(near, own, far, wsum, devices * mem_dev)
-    parts = apply_roots(roots, rhs, columns)
+    high, low, weight, _ = inverse_roots(near, own, far, wsum, devices * mem_dev)
+    parts = apply_roots(high, low, weight, columns)
     return restore(lax.all_to_all(parts, "mem", 0, 0, tiled=True))
 
 

time: 104 us -> 113 us (1.087)
  waiting for transfers between devices: 2.16 us -> 5.93 us
  blocking collectives: 55.6 us -> 58.9 us
  local copies, waits for them, and re-layouts: 2.95 us -> 4.78 us
    ppermute x1, waiting for transfers between devices: 2.13 us -> 5.9 us  [neighbours(): near = lax.ppermute(value, ('mem', 'tile'), pairs)]
    all_to_all x1, blocking collectives: 32.7 us -> 36 us  [on_device(): return restore(lax.all_to_all(parts, 'mem', 0, 0, tiled=True))]
    unnamed x11 -> x15, local copies, waits for them, and re-layouts: 1.24 us -> 3.07 us
  transfers between devices with their start and end apart: 4 -> 4, of which waited for: 1 -> 1; matrix products, arithmetic and copies ran while one was open for 2% -> 2% of each run, Pallas kernels for 25% -> 23%
where the time goes in v4:
time: 113 us
  blocking collectives  58.9 us (52%)
  Pallas kernels  28.9 us (26%)
  starting transfers between devices  12.6 us (11%)
  waiting for transfers between devices  5.93 us (5%)
  local copies, waits for them, and re-layouts  4.78 us (4%)
  other arithmetic  1.26 us (1%)
    all_to_all x1, blocking collectives, on_device(): return restore(lax.all_to_all(parts, 'mem', 0, 0, tiled=True))  36 us
    all_gather x1, blocking collectives, on_device(): own = lax.all_gather(message, 'mem', axis=0, tiled=True)  22.9 us
    pallas_call x1, Pallas kernels, inverse_roots(): pl.pallas_call(root_kernel, out_shape=(jax.ShapeDtypeStruct(square, BF),...  21.1 us
    ppermute x1, waiting for transfers between devices, neighbours(): near = lax.ppermute(value, ('mem', 'tile'), pairs)  5.9 us
    all_to_all x1, starting transfers between devices, on_device(): lax.all_to_all(field.reshape(devices, lines // devices, levels, mem_dev,...  3.8 us
    ppermute x1, starting transfers between devices, neighbours(): far = lax.ppermute(near, 'mem', [(m, m ^ 1) for m in range(mem)])  3.78 us
    unnamed x15, local copies, waits for them, and re-layouts  3.07 us
    ppermute x1, starting transfers between devices, neighbours(): near = lax.ppermute(value, ('mem', 'tile'), pairs)  2.77 us
  transfers between devices with their start and end apart: 4, of which 1 were waited for; matrix products, arithmetic and copies ran while one was open for 2% of the time, Pallas kernels for 23%

profile of v4, /device:TPU:1, one launch (start us, length us, event | category | flops | bytes accessed | tf_op | source)
XLA Modules:
  0.0 112.7 jit_solution(2869475631808331856)
XLA Ops:
  0.0 1.0 slice.3
  1.0 2.2 %collective-permute-start = (f32[2,2,32,128]{3,2,1,0:T(8,128)S(1)}, f32[2,2,32,128]{3,2,1,0:T(8,128)S(1)}, u32[]{:S(2)}, u32[]{:S(2)}) collective-permute-start(f32[2,2,32,128]{3,2,1,0:T(8,128)S(1)} %bitcast.11), channel_id=1, source_target_pairs={{0,1},{1,2},{2,3},{3,4},{4,5},{5,6},{6,7},{7,8},{8,9},{9,10},{10,1... | collective-permute-start | bytes 196616 | tf_op jit(solution)/shard_map/ppermute | solution.py:517
  3.2 0.7 convert_element_type.3
  3.9 0.7 concatenate.3.pack_ref
  4.6 0.0 copy-start
  4.6 1.2 %copy-done = f32[32,2,32,128]{3,2,1,0:T(8,128)S(1)} copy-done((f32[32,2,32,128]{3,2,1,0:T(8,128)S(1)}, f32[32,2,32,128]{3,2,1,0:T(8,128)}, u32[]{:S(2)}) %copy-start) | copy-done | bytes 1048600
  5.8 2.6 %shard_map.91 = (f32[32,2,32,128]{3,2,1,0:T(8,128)}, f32[2,2,32,128]{3,2,1,0:T(8,128)S(1)}, f32[32,256]{1,0:T(8,128)S(1)}) custom-call(f32[2048,128]{1,0:T(8,128)S(1)} %bitcast.10, f32[8,256]{1,0:T(8,128)S(1)} %concatenate.3.pack_ref), custom_call_target="tpu_custom_call" | custom-call | flops 100000000 | bytes 2000000 | tf_op jit(solution)/shard_map/pallas_call | solution.py:421
  8.5 0.0 copy-start.5
  8.5 0.0 collective-permute-done.halo_ref
  8.5 0.8 shard_map.92
  9.3 22.9 %all_gather.3.block_ref = f32[512,256]{1,0:T(8,128)S(1)} all-gather(f32[32,256]{1,0:T(8,128)S(1)} %get-tuple-element.26), channel_id=1, replica_groups=mesh['mem'=16,'tile'=16] {'mem'}, dimensions={0}, use_global_device_ids=true | all-gather | bytes 557056 | tf_op jit(solution)/shard_map/all_gather | solution.py:545
  32.2 3.8 %all-to-all-start = ((f32[16,2,2,32,128]{4,3,2,1,0:T(8,128)}), f32[16,2,2,32,128]{4,3,2,1,0:T(8,128)S(1)}, u32[]{:S(2)}, u32[]{:S(2)}) async-start(f32[16,2,2,32,128]{4,3,2,1,0:T(8,128)} %bitcast.6), calls=%async_computation | async-start | bytes 2097152 | tf_op jit(solution)/shard_map/all_to_all | solution.py:550
  36.0 2.8 %collective-permute-start.1 = (f32[512,256]{1,0:T(8,128)S(1)}, f32[512,256]{1,0:T(8,128)S(1)}, u32[]{:S(2)}, u32[]{:S(2)}) collective-permute-start(f32[512,256]{1,0:T(8,128)S(1)} %all_gather.3.block_ref), channel_id=1, source_target_pairs={{0,1},{1,2},{2,3},{3,4},{4,5},{5,6},{6,7},{7,8},{8,9},{9,10},{10,1... | collective-permute-start | bytes 1572872 | tf_op jit(solution)/shard_map/ppermute | solution.py:527
  38.8 0.0 copy-done.3
  38.8 0.0 copy-done.5
  38.8 0.1 select_reduce_fusion.1
  38.9 0.0 copy-done.4
  38.9 0.0 copy-done.6
  38.9 0.1 compare_select_fusion.2
  39.0 5.9 %collective-permute-done.1.block_ref = f32[512,256]{1,0:T(8,128)S(1)} collective-permute-done((f32[512,256]{1,0:T(8,128)S(1)}, f32[512,256]{1,0:T(8,128)S(1)}, u32[]{:S(2)}, u32[]{:S(2)}) %collective-permute-start.1) | collective-permute-done | bytes 524320 | tf_op jit(solution)/shard_map/ppermute | solution.py:527
  44.9 3.8 %collective-permute-start.2 = (f32[512,256]{1,0:T(8,128)S(1)}, f32[512,256]{1,0:T(8,128)S(1)}, u32[]{:S(2)}, u32[]{:S(2)}) collective-permute-start(f32[512,256]{1,0:T(8,128)S(1)} %collective-permute-done.1.block_ref), channel_id=1, source_target_pairs={{0,16},{16,0},{32,48},{48,32},{64,80},{80,64},{96,112},{112,96},{1... | collective-permute-start | bytes 1572872 | tf_op jit(solution)/shard_map/ppermute | solution.py:528
  48.7 0.4 select_reduce_fusion.wsum_ref
  49.1 0.8 shard_map.93
  49.9 0.9 shard_map.94
  50.8 0.0 collective-permute-done.2.far_ref
  50.8 21.1 %shard_map.95 = (bf16[2,512,512]{2,1,0:T(8,128)(2,1)S(1)}, bf16[2,512,512]{2,1,0:T(8,128)(2,1)S(1)}, f32[2,512,1]{2,1,0:T(8,128)S(1)}, f32[2,8,512]{2,1,0:T(8,128)}) custom-call(f32[512,256]{1,0:T(8,128)S(1)} %collective-permute-done.2.far_ref, f32[2,768]{1,0:T(2,128)S(1)} %select_reduce_fusion.wsum_ref, f32[2,512,512]{2,1,0:T(8,128)S(1)} %get-tuple-element.35.gram_ref, ...), custom_call_target="tpu_custom_call" | custom-call | flops 24999999488 | bytes 4000000 | tf_op jit(solution)/shard_map/pallas_call | solution.py:328
  71.9 0.8 copy-done.1
  72.7 0.0 all-to-all-done.cols_ref
  72.7 1.0 copy-done.2
  73.7 1.2 %shard_map.96 = f32[16,2,2,32,128]{4,3,2,1,0:T(8,128)S(1)} custom-call(bf16[2,512,512]{2,1,0:T(8,128)(2,1)S(1)} %get-tuple-element.37.high_ref, bf16[2,512,512]{2,1,0:T(8,128)(2,1)S(1)} %get-tuple-element.38.low_ref, f32[2,512,1]{2,1,0:T(8,128)S(1)} %copy-done.2, f32[16,2,2,32,128]{4,3,2,1,0:T(8,128)S(1)} %all-to-all-done.cols_ref), custom_call_target="tpu_custom_call" | custom-call | flops 800000000 | bytes 4000000 | tf_op jit(solution)/shard_map/pallas_call | solution.py:372
  74.9 36.0 %all_to_all.10.part_ref = f32[16,2,2,32,128]{4,3,2,1,0:T(8,128)S(1)} all-to-all(f32[16,2,2,32,128]{4,3,2,1,0:T(8,128)S(1)} %shard_map.96), channel_id=1, replica_groups=mesh['mem'=16,'tile'=16] {'mem'}, dimensions={0} | all-to-all | bytes 2097152 | tf_op jit(solution)/shard_map/all_to_all | solution.py:566
  110.9 1.6 %shard_map.97 = f32[2048,128]{1,0:T(8,128)} custom-call(f32[16,2,2,32,128]{4,3,2,1,0:T(8,128)S(1)} %all_to_all.10.part_ref), custom_call_target="tpu_custom_call" | custom-call | tf_op jit(solution)/shard_map/pallas_call | solution.py:500
  (8 shorter events, 0.0 us)
Async XLA Ops:
  1.0 7.5 %collective-permute-start = (f32[2,2,32,128]{3,2,1,0:T(8,128)S(1)}, f32[2,2,32,128]{3,2,1,0:T(8,128)S(1)}, u32[]{:S(2)}, u32[]{:S(2)}) collective-permute-start(f32[2,2,32,128]{3,2,1,0:T(8,128)S(1)} %bitcast.11), channel_id=1, source_target_pairs={{0,1},{1,2},{2,3},{3,4},{4,5},{5,6},{6,7},{7,8},{8,9},{9,10},{10,1... | collective-permute-start | bytes 196616 | tf_op jit(solution)/shard_map/ppermute | solution.py:517
  4.6 1.2 %copy-start = (f32[32,2,32,128]{3,2,1,0:T(8,128)S(1)}, f32[32,2,32,128]{3,2,1,0:T(8,128)}, u32[]{:S(2)}) copy-start(f32[32,2,32,128]{3,2,1,0:T(8,128)} %param.9) | copy-start | bytes 3145732
  8.5 30.3 %copy-start.3 = (s32[2,512]{1,0:T(2,128)S(1)}, s32[2,512]{1,0:T(2,128)}, u32[]{:S(2)}) copy-start(s32[2,512]{1,0:T(2,128)} %param.15) | copy-start | bytes 12292
  8.5 30.3 %copy-start.5 = (f32[16]{0:T(128)S(1)}, f32[16]{0:T(128)}, u32[]{:S(2)}) copy-start(f32[16]{0:T(128)} %param.17) | copy-start | bytes 196
  8.5 30.4 %copy-start.4 = (s32[2,512]{1,0:T(2,128)S(1)}, s32[2,512]{1,0:T(2,128)}, u32[]{:S(2)}) copy-start(s32[2,512]{1,0:T(2,128)} %param.14) | copy-start | bytes 12292
  8.5 30.5 %copy-start.6 = (s32[2]{0:T(128)S(1)}, s32[2]{0:T(128)}, u32[]{:S(2)}) copy-start(s32[2]{0:T(128)} %param.16) | copy-start | bytes 28
  32.2 40.5 %all-to-all-start = ((f32[16,2,2,32,128]{4,3,2,1,0:T(8,128)}), f32[16,2,2,32,128]{4,3,2,1,0:T(8,128)S(1)}, u32[]{:S(2)}, u32[]{:S(2)}) async-start(f32[16,2,2,32,128]{4,3,2,1,0:T(8,128)} %bitcast.6), calls=%async_computation | async-start | bytes 2097152 | tf_op jit(solution)/shard_map/all_to_all | solution.py:550
  36.0 8.9 %collective-permute-start.1 = (f32[512,256]{1,0:T(8,128)S(1)}, f32[512,256]{1,0:T(8,128)S(1)}, u32[]{:S(2)}, u32[]{:S(2)}) collective-permute-start(f32[512,256]{1,0:T(8,128)S(1)} %all_gather.3.block_ref), channel_id=1, source_target_pairs={{0,1},{1,2},{2,3},{3,4},{4,5},{5,6},{6,7},{7,8},{8,9},{9,10},{10,1... | collective-permute-start | bytes 1572872 | tf_op jit(solution)/shard_map/ppermute | solution.py:527
  44.9 5.9 %collective-permute-start.2 = (f32[512,256]{1,0:T(8,128)S(1)}, f32[512,256]{1,0:T(8,128)S(1)}, u32[]{:S(2)}, u32[]{:S(2)}) collective-permute-start(f32[512,256]{1,0:T(8,128)S(1)} %collective-permute-done.1.block_ref), channel_id=1, source_target_pairs={{0,16},{16,0},{32,48},{48,32},{64,80},{80,64},{96,112},{112,96},{1... | collective-permute-start | bytes 1572872 | tf_op jit(solution)/shard_map/ppermute | solution.py:528
  71.9 0.8 copy-start.1
  72.7 1.0 copy-start.2
